TPU v7x, 512 devices: a whole 4x4x16 slice. The times are simulated.
512 devices in a mesh: tile: 64 (over x, z), rep: 8 (over y, core).
Axes of the slice: x: 4, y: 4, z: 16, core: 2. Of those that a mesh axis runs over, the one named last changes fastest.
Arguments:
- owner: int32 [262144, 1], P(('tile', 'rep')), may hold values from 0 to 63; in each aligned block of 512 rows (0 to 511, 512 to 1023, ...) at most 24 rows name the same one
- tile_local: int32 [262144], P(('tile', 'rep')), may hold values from 0 to 15
- anchor: int32 [262144], P(('tile', 'rep')), may hold values from 0 to 224
- frac_x: int32 [262144], P(('tile', 'rep')), may hold values from 0 to 255
- frac_y: int32 [262144], P(('tile', 'rep')), may hold values from 0 to 255
- label: int32 [262144], P(('tile', 'rep')), may hold values 0 or 1
- raster: bfloat16 [1024, 64, 256], P('tile'), may hold values from -6 to 6
- beta: float32 [512], replicated, may hold values from -0.9 to 0.9
- smooth: float32 [64], replicated, may hold values from 0.002 to 0.05
Outputs:
- beta_new: float32 [512], replicated
- eta_new: float32 [262144], P(('tile', 'rep'))
Inputs may be any that keep to these rules, and one draw needn't show every extreme that they name: Among the 512 fixes of one device no owner is named more than 24 times, and 24 is reached for some owner. The square's lower-left cell is row anchor // 15 and column anchor mod 15 of the tile, so the whole square lies inside the tile.
All inputs are finite; a program needn't handle non-finite values. No bound on the sum of `label` on one device may be relied on, other than what follows from the above.
Results may differ from a plain program's by a relative error of at most 0.0033.
Values may be sent and summed in bfloat16 or wider, within the bound.
A program may use at most 128 MiB of HBM per device.

v0:
```python
import jax
import jax.numpy as jnp
from jax import lax
from jax.sharding import PartitionSpec as P

SPLINES = 8


RIDGE = 0.002


def interpolate(raster, tiles, anchors, frac_x, frac_y):
    row_id = anchors // 15
    corner = row_id * 16 + (anchors - row_id * 15)
    weight_x = frac_x.astype(jnp.float32)
    weight_y = frac_y.astype(jnp.float32)
    lower_left = raster[tiles, :, corner].astype(jnp.float32)
    lower_right = raster[tiles, :, corner + 1].astype(jnp.float32)
    upper_left = raster[tiles, :, corner + 16].astype(jnp.float32)
    upper_right = raster[tiles, :, corner + 17].astype(jnp.float32)
    total = ((256.0 - weight_x) * (256.0 - weight_y))[..., None] * lower_left
    total = total + (weight_x * (256.0 - weight_y))[..., None] * lower_right
    total = total + ((256.0 - weight_x) * weight_y)[..., None] * upper_left
    total = total + (weight_x * weight_y)[..., None] * upper_right
    return total / 65536.0


def expand(values):
    knots = 0.5 * (jnp.arange(SPLINES, dtype=jnp.float32) - (SPLINES - 1) / 2.0)
    bumps = jnp.maximum(1.0 - jnp.abs(values[..., None] - knots) / 0.75, 0.0) ** 3
    return bumps.reshape(values.shape[:-1] + (values.shape[-1] * SPLINES,)).astype(jnp.bfloat16)


def normal_terms(rows, beta, outcome, live):
    rows_wide = rows.astype(jnp.float32)
    eta = jnp.dot(rows_wide, beta, precision=lax.Precision.HIGHEST)
    prob = jax.nn.sigmoid(eta)
    weight = prob * (1.0 - prob) * live
    scaled = (jnp.sqrt(weight)[:, None] * rows_wide).astype(jnp.bfloat16)
    gram = jnp.dot(scaled.T, scaled, preferred_element_type=jnp.float32)
    resid = weight * eta + (outcome - prob) * live
    target = jnp.dot(resid, rows_wide, precision=lax.Precision.HIGHEST)
    return (gram, target)


def penalty(smooth):
    first = jnp.arange(SPLINES - 2)[:, None]
    cols = jnp.arange(SPLINES)[None, :]
    second = (
        (cols == first).astype(jnp.float32)
        - 2.0 * (cols == first + 1).astype(jnp.float32)
        + (cols == first + 2).astype(jnp.float32)
    )
    inner = jnp.dot(second.T, second, precision=lax.Precision.HIGHEST)
    layers = smooth.shape[0]
    blocks = (
        jnp.eye(layers, dtype=jnp.float32)[:, None, :, None]
        * smooth[:, None, None, None]
        * inner[None, :, None, :]
    )
    return blocks.reshape(layers * SPLINES, layers * SPLINES)


def solve_step(gram, target, smooth, count):
    system = gram / count + penalty(smooth) + RIDGE * jnp.eye(gram.shape[0], dtype=jnp.float32)
    factor = jnp.linalg.cholesky(system)
    return jax.scipy.linalg.cho_solve((factor, True), target / count)


def place_slots(owners, owner_count):
    match = (owners[:, None] == jnp.arange(owner_count, dtype=jnp.int32)[None, :]).astype(jnp.int32)
    before = jnp.cumsum(match, axis=0) - match
    return jnp.sum(before * match, axis=1)


def pack_fields(fields, owners, slots, owner_count, capacity):
    stacked = jnp.stack(fields)
    empty = jnp.zeros((len(fields), owner_count, capacity), jnp.int32)
    return empty.at[:, owners, slots].set(stacked)


def shards(owner, tile_local, anchor, frac_x, frac_y, label, raster, beta, smooth):
    owners = owner[:, 0]
    tok_rows = owners.shape[0]
    owner_count = lax.axis_size("tile")
    capacity = 3 * tok_rows // owner_count
    count = float(tok_rows * owner_count * lax.axis_size("rep"))
    slots = place_slots(owners, owner_count)
    codes = pack_fields((tile_local, anchor, frac_x, frac_y), owners, slots, owner_count, capacity)
    arrived = lax.all_to_all(codes, "tile", split_axis=1, concat_axis=1, tiled=True)
    values = interpolate(raster, arrived[0], arrived[1], arrived[2], arrived[3])
    returned = lax.all_to_all(expand(values), "tile", split_axis=0, concat_axis=0, tiled=True)
    rows = returned[owners, slots]
    gram, target = normal_terms(
        rows, beta, label.astype(jnp.float32), jnp.ones((tok_rows,), jnp.float32)
    )
    gram, target = lax.psum((gram, target), ("tile", "rep"))
    beta_new = solve_step(gram, target, smooth, count)
    eta_new = jnp.dot(rows.astype(jnp.float32), beta_new, precision=lax.Precision.HIGHEST)
    return (beta_new, eta_new)


def solution(mesh):
    placed = (
        P(("tile", "rep"), None),
        P(("tile", "rep")),
        P(("tile", "rep")),
        P(("tile", "rep")),
        P(("tile", "rep")),
        P(("tile", "rep")),
        P("tile", None, None),
        P(),
        P(),
    )
    return jax.shard_map(
        shards, mesh=mesh, in_specs=placed, out_specs=(P(), P(("tile", "rep"))), check_vma=False
    )
```

profile of v0, /device:TPU:1, one launch (start us, length us, event | category | flops | bytes accessed | tf_op | source)
XLA Modules:
  0.0 819.5 jit_solution(16097744920794348568)
XLA Ops:
  7.2 0.8 fusion.33
  7.9 1.2 reduce-window.6
  9.4 0.8 fusion.28
  10.2 0.7 or_select_fusion
  10.9 0.7 add_bitcast_fusion.1
  11.9 24.2 %scatter_fusion = s32[4,64,24]{0,2,1:T(8,128)S(1)} fusion(s32[4,64,24]{0,2,1:T(8,128)S(1)} %broadcast_in_dim.4, s32[512]{0:T(512)S(1)} %bitcast.253, s32[512,4]{1,0:T(8,128)S(1)} %copy.88), kind=kCustom, calls=%fused_computation.5 | custom fusion | bytes 28672 | tf_op jit(solution)/shard_map/scatter | solution.py:79
  36.1 1.1 copy.89
  37.1 19.1 %all-to-all-start = ((s32[4,64,24]{2,0,1:T(4,128)}), s32[4,64,24]{2,0,1:T(4,128)S(1)}, u32[]{:S(2)}, u32[]{:S(2)}) async-start(s32[4,64,24]{2,0,1:T(4,128)} %copy.89), calls=%async_computation | async-start | bytes 262144 | tf_op jit(solution)/shard_map/all_to_all | solution.py:90
  56.2 0.5 copy.96
  56.9 13.3 %all-to-all-done = s32[4,64,24]{2,0,1:T(4,128)S(1)} async-done(((s32[4,64,24]{2,0,1:T(4,128)}), s32[4,64,24]{2,0,1:T(4,128)S(1)}, u32[]{:S(2)}, u32[]{:S(2)}) %all-to-all-start) | async-done | bytes 24608 | tf_op jit(solution)/shard_map/all_to_all | solution.py:90
  70.8 8.5 %gather_fusion.3 = bf16[1536,64]{1,0:T(8,128)(2,1)S(1)} fusion(bf16[16,64,256]{1,2,0:T(8,128)(2,1)S(1)} %copy.96, s32[1536]{0:T(1024)S(1)} %reshape.460), kind=kCustom, calls=%fused_computation.3 | custom fusion | bytes 405504 | tf_op jit(solution)/shard_map/gather | solution.py:20
  79.3 8.5 %gather_fusion.2 = bf16[1536,64]{1,0:T(8,128)(2,1)S(1)} fusion(bf16[16,64,256]{1,2,0:T(8,128)(2,1)S(1)} %copy.96, s32[1536]{0:T(1024)S(1)} %reshape.454), kind=kCustom, calls=%fused_computation.2 | custom fusion | bytes 405504 | tf_op jit(solution)/shard_map/gather | solution.py:19
  88.0 8.5 %gather_fusion.1 = bf16[1536,64]{1,0:T(8,128)(2,1)S(1)} fusion(bf16[16,64,256]{1,2,0:T(8,128)(2,1)S(1)} %copy.96, s32[1536]{0:T(1024)S(1)} %reshape.448), kind=kCustom, calls=%fused_computation.1 | custom fusion | bytes 405504 | tf_op jit(solution)/shard_map/gather | solution.py:18
  96.6 8.5 %gather_fusion = bf16[1536,64]{1,0:T(8,128)(2,1)S(1)} fusion(bf16[16,64,256]{1,2,0:T(8,128)(2,1)S(1)} %copy.96, s32[1536]{0:T(1024)S(1)} %reshape.442), kind=kCustom, calls=%fused_computation | custom fusion | bytes 405504 | tf_op jit(solution)/shard_map/gather | solution.py:17
  105.6 1.0 fusion.15
  106.6 0.3 copy.106
  106.9 3.1 broadcast_bitcast_fusion
  110.0 5.0 copy.107
  115.0 2.0 fusion
  116.9 7.6 all-to-all-start.1
  124.6 12.2 %all-reduce.3.cloned.1.call-start = ((), (), s32[]{:S(2)}) async-start(), calls=%async_computation.2 | async-start | bytes 2097152 | tf_op jit(solution)/shard_map/psum | solution.py:97
  137.1 7.9 broadcast_multiply_fusion
  145.1 13.4 %mul.212 = f32[512,512]{1,0:T(8,128)} reshape(f32[64,8,64,8]{3,2,1,0:T(8,128)} %broadcast_multiply_fusion) | data formatting | bytes 2097152 | tf_op jit(solution)/shard_map/mul | solution.py:57
  158.5 1.6 copy.109
  160.1 34.9 %all-to-all-done.1 = bf16[64,24,512]{2,1,0:T(8,128)(2,1)S(1)} async-done(((bf16[64,24,512]{2,1,0:T(8,128)(2,1)}), bf16[64,24,512]{2,1,0:T(8,128)(2,1)S(1)}, u32[]{:S(2)}, u32[]{:S(2)}) %all-to-all-start.1) | async-done | bytes 1572896 | tf_op jit(solution)/shard_map/all_to_all | solution.py:92
  194.9 3.9 gather_fusion.4
  198.8 0.5 fusion.105
  199.4 1.7 fusion.18
  201.1 0.3 fusion.106
  201.4 106.7 %psum.15 = f32[512]{0:T(512)S(1)} all-reduce(f32[512]{0:T(512)S(1)} %bitcast.264), channel_id=1, replica_groups=mesh['tile'=64,'rep'=8] {'tile','rep'}, use_global_device_ids=true, to_apply=%region_13.14 | all-reduce | flops 512 | bytes 4096 | tf_op jit(solution)/shard_map/psum | solution.py:97
  308.2 359.3 %all-reduce.3.cloned.1.call-done = f32[512,512]{0,1:T(8,128)} async-done(((f32[512,512]{0,1:T(8,128)}), f32[512,512]{0,1:T(8,128)}) %all-reduce.3.cloned.1.call-update) | async-done | bytes 1048592 | tf_op jit(solution)/shard_map/psum | solution.py:97
  667.5 1.4 select_add_fusion
  668.9 0.3 copy.110
  669.5 1.0 copy-done.1
  670.4 11.7 %cholesky.103 = f32[128,128]{1,0:T(8,128)S(1)} custom-call(f32[128,128]{1,0:T(8,128)S(1)} %cholesky.263), custom_call_target="Cholesky" | custom-call | tf_op jit(solution)/shard_map/jit(cholesky)/cholesky | solution.py:66
  682.3 9.8 %custom-call.34 = f32[1,128,128]{1,2,0:T(8,128)S(1)} custom-call(f32[1,128,128]{2,1,0:T(8,128)S(1)} %get-tuple-element.47), custom_call_target="InvertDiagBlocksLowerTriangular" | custom-call | tf_op jit(solution)/shard_map/jit(cholesky)/cholesky | solution.py:66
  692.1 1.2 fusion.24
  693.5 1.3 convolution_subtract_fusion
  694.8 11.7 %cholesky.215 = f32[128,128]{1,0:T(8,128)S(1)} custom-call(f32[128,128]{1,0:T(8,128)S(1)} %cholesky.267), custom_call_target="Cholesky" | custom-call | tf_op jit(solution)/shard_map/jit(cholesky)/cholesky | solution.py:66
  706.6 10.0 %custom-call.35 = f32[1,128,128]{1,2,0:T(8,128)S(1)} custom-call(f32[1,128,128]{2,1,0:T(8,128)S(1)} %get-tuple-element.45), custom_call_target="InvertDiagBlocksLowerTriangular" | custom-call | tf_op jit(solution)/shard_map/jit(cholesky)/cholesky | solution.py:66
  716.8 0.3 convolution_dynamic-update-slice_fusion
  717.1 1.5 convolution_subtract_fusion.1
  718.6 11.7 %cholesky.236 = f32[128,128]{1,0:T(8,128)S(1)} custom-call(f32[128,128]{1,0:T(8,128)S(1)} %cholesky.272), custom_call_target="Cholesky" | custom-call | tf_op jit(solution)/shard_map/jit(cholesky)/cholesky | solution.py:66
  730.5 9.8 %custom-call.36 = f32[1,128,128]{1,2,0:T(8,128)S(1)} custom-call(f32[1,128,128]{2,1,0:T(8,128)S(1)} %get-tuple-element.43), custom_call_target="InvertDiagBlocksLowerTriangular" | custom-call | tf_op jit(solution)/shard_map/jit(cholesky)/cholesky | solution.py:66
  740.3 0.3 convolution_dynamic-update-slice_fusion.1
  740.6 1.3 convolution_subtract_fusion.2
  741.9 11.9 %cholesky.253 = f32[128,128]{1,0:T(8,128)S(1)} custom-call(f32[128,128]{1,0:T(8,128)S(1)} %convolution_subtract_fusion.2), custom_call_target="Cholesky" | custom-call | tf_op jit(solution)/shard_map/jit(cholesky)/cholesky | solution.py:66
  754.0 0.6 compare_reduce_fusion.3
  754.6 0.7 compare_reduce_fusion.2
  755.3 0.6 compare_reduce_fusion.1
  756.0 0.7 compare_reduce_fusion
  759.3 8.9 %while.1 = (s32[]{:T(128)}, f32[512,512]{0,1:T(8,128)S(1)}, s32[4,2]{0,1:T(2,128)S(1)}, f32[4,128,128]{2,1,0:T(8,128)S(1)}, s32[]{:T(128)}) while((s32[]{:T(128)}, f32[512,512]{0,1:T(8,128)S(1)}, s32[4,2]{0,1:T(2,128)S(1)}, f32[4,128,128]{2,1,0:T(8,128)S(1)}, s32[]{:T(128)}) %tuple.42), condition=%wide.while_cond, body=%wide.while_body.sunk | while | flops 2 | bytes 393329 | solution.py:67
  759.4 0.6 fusion.122
  760.0 1.4 dynamic-slice.7
  761.6 0.6 fusion.122
  762.2 1.4 dynamic-slice.7
  763.9 0.6 fusion.122
  764.5 1.4 dynamic-slice.7
  766.1 0.6 fusion.122
  766.7 1.4 dynamic-slice.7
  768.3 39.3 %custom-call.37 = f32[4,128,128]{1,2,0:T(8,128)S(1)} custom-call(f32[4,128,128]{2,1,0:T(8,128)S(1)} %get-tuple-element.9), custom_call_target="InvertDiagBlocksLowerTriangular" | custom-call | tf_op jit(solution)/shard_map/jit(_cho_solve)/triangular_solve | solution.py:67
  809.9 0.3 fusion.10
  810.5 0.6 pad_maximum_fusion
  811.1 1.1 fusion.101
  (89 shorter events, 6.9 us)
Async XLA Ops:
  7.2 191.7 %copy-start = (f32[512]{0:T(512)S(1)}, f32[512]{0:T(512)}, u32[]{:S(2)}) copy-start(f32[512]{0:T(512)} %param.16) | copy-start | bytes 6148
  7.2 49.1 %copy-start.2 = (bf16[16,64,256]{2,1,0:T(8,128)(2,1)S(1)}, bf16[16,64,256]{2,1,0:T(8,128)(2,1)}, u32[]{:S(2)}) copy-start(bf16[16,64,256]{2,1,0:T(8,128)(2,1)} %param.15) | copy-start | bytes 1572868
  37.1 33.1 %all-to-all-start = ((s32[4,64,24]{2,0,1:T(4,128)}), s32[4,64,24]{2,0,1:T(4,128)S(1)}, u32[]{:S(2)}, u32[]{:S(2)}) async-start(s32[4,64,24]{2,0,1:T(4,128)} %copy.89), calls=%async_computation | async-start | bytes 262144 | tf_op jit(solution)/shard_map/all_to_all | solution.py:90
  115.0 22.1 %copy-start.4 = (f32[64]{0:T(128)S(1)}, f32[64]{0:T(128)}, u32[]{:S(2)}) copy-start(f32[64]{0:T(128)} %param.17) | copy-start | bytes 772
  116.9 78.0 %all-to-all-start.1 = ((bf16[64,24,512]{2,1,0:T(8,128)(2,1)}), bf16[64,24,512]{2,1,0:T(8,128)(2,1)S(1)}, u32[]{:S(2)}, u32[]{:S(2)}) async-start(bf16[64,24,512]{2,1,0:T(8,128)(2,1)} %fusion), calls=%async_computation.1 | async-start | bytes 3145728 | tf_op jit(solution)/shard_map/all_to_all | solution.py:92
  124.6 542.9 %all-reduce.3.cloned.1.call-start = ((), (), s32[]{:S(2)}) async-start(), calls=%async_computation.2 | async-start | bytes 2097152 | tf_op jit(solution)/shard_map/psum | solution.py:97
  160.1 39.3 %copy-start.3 = (s32[512]{0:T(512)S(1)}, s32[512]{0:T(512)}, u32[]{:S(2)}) copy-start(s32[512]{0:T(512)} %param.14) | copy-start | bytes 6148
  669.4 1.0 copy-start.1
Sparse Core Ops, SparseCore 0:
  201.3 466.1 all-reduce.2
where the time goes:
time: 827 us; the launch traced here: 820 us
  waiting for transfers between devices  408 us (49%)
  other arithmetic  136 us (16%)
  blocking collectives  107 us (13%)
  local copies, waits for them, and re-layouts  99.6 us (12%)
  starting transfers between devices  38.9 us (5%)
  between operations  17.5 us (2%)
  matrix products  12.7 us (2%)
    psum x1, waiting for transfers between devices, shards(): gram, target = lax.psum((gram, target), ('tile', 'rep'))  359 us
    psum x1, blocking collectives, shards(): gram, target = lax.psum((gram, target), ('tile', 'rep'))  107 us
    another operation x15, other arithmetic, solve_step(): factor = jnp.linalg.cholesky(system)  79.4 us
    another operation x4, other arithmetic, solve_step(): return jax.scipy.linalg.cho_solve((factor, True), target / count)  40.1 us
    all_to_all x1, waiting for transfers between devices, shards(): lax.all_to_all(expand(values), 'tile', split_axis=0, concat_axis=0, tiled...  34.9 us
    scatter x2, local copies, waits for them, and re-layouts, pack_fields(): return empty.at[:, owners, slots].set(stacked)  25.2 us
    all_to_all x1, starting transfers between devices, shards(): lax.all_to_all(codes, 'tile', split_axis=1, concat_axis=1, tiled=True)  19.1 us
  transfers between devices with their start and end apart: 3, of which 3 were waited for; matrix products, arithmetic and copies ran while one was open for 3% of the time, Pallas kernels for 0%

commit v1 on v0

v1 whole, which is shorter than its diff:
```python
import functools

import jax
import jax.numpy as jnp
from jax import lax
from jax.experimental import pallas as pl
from jax.experimental.pallas import tpu as pltpu
from jax.sharding import PartitionSpec as P

SPLINES = 8
RIDGE = 0.002
LAYERS = 64
BASIS = 512
FIXES = 512
SLOTS = 24
OWNERS = 64
PLANE = 16
DEEP = 16
ROWS = 48
MESH = pl.DeviceIdType.MESH
HIGHEST = lax.Precision.HIGHEST
VMEM = pl.BlockSpec(memory_space=pltpu.VMEM)
SMEM = pl.BlockSpec(memory_space=pltpu.SMEM)
LIMIT = 48 * 1024 * 1024
BLOCKS = [(i, j) for i in range(4) for j in range(i, 4)]
NT = (((1,), (1,)), ((), ()))
TN = (((0,), (0,)), ((), ()))


def dot(a, b, dims=(((1,), (0,)), ((), ())), precision=None):
    return lax.dot_general(a, b, dims, precision=precision, preferred_element_type=jnp.float32)


def iota(shape, axis):
    return lax.broadcasted_iota(jnp.int32, shape, axis)


def thirds(x):
    high = x.astype(jnp.bfloat16)
    rest = x - high.astype(jnp.float32)
    mid = rest.astype(jnp.bfloat16)
    low = (rest - mid.astype(jnp.float32)).astype(jnp.bfloat16)
    return high, mid, low


def stacked_thirds(x):
    high, mid, low = thirds(x)
    row = iota((16, x.shape[1]), 0)
    wide = lambda part: jnp.broadcast_to(part.astype(jnp.float32), row.shape)
    parts = jnp.where(row == 0, wide(high), jnp.where(row == 1, wide(mid), jnp.where(row == 2, wide(low), 0.0)))
    return parts.astype(jnp.bfloat16)


def position():
    return lax.axis_index("tile"), lax.axis_index("rep")


def request_rows(owner, local, anchor, frac_x, frac_y, label):
    named = (iota((OWNERS, FIXES), 0) == owner).astype(jnp.float32)
    named_b = named.astype(jnp.bfloat16)
    earlier = (iota((FIXES, FIXES), 0) < iota((FIXES, FIXES), 1)).astype(jnp.float32).astype(jnp.bfloat16)
    before = dot(named_b, earlier)
    slot = jnp.sum(before * named, axis=0, keepdims=True)
    at = iota((SLOTS, FIXES), 0).astype(jnp.float32) == slot
    fields = [field.astype(jnp.float32) for field in (local, anchor, frac_x, frac_y, label + 1)]
    spread = [jnp.where(at, field, 0.0) for field in fields] + [jnp.zeros((8, FIXES), jnp.float32)]
    spread = jnp.concatenate(spread, axis=0).astype(jnp.bfloat16)
    return dot(named_b, spread, NT), slot


def greet_tile(barrier, tile, rep):
    def greet(step, _):
        pl.semaphore_signal(barrier, inc=1, device_id=(lax.rem(tile + step, OWNERS), rep), device_id_type=MESH)
        return 0

    lax.fori_loop(1, OWNERS, greet, 0)


def exchange(tile, rep, out, came, send_sem, recv_sem):
    def copy(peer, slot):
        return pltpu.make_async_remote_copy(
            src_ref=out.at[peer], dst_ref=came.at[slot], send_sem=send_sem.at[peer], recv_sem=recv_sem.at[slot],
            device_id=(peer, rep), device_id_type=MESH)

    def begin(step, _):
        copy(lax.rem(tile + step, OWNERS), tile).start()
        return 0

    def finish(step, _):
        peer = lax.rem(tile + step, OWNERS)
        copy(peer, peer).wait_recv()
        copy(peer, peer).wait_send()
        return 0

    lax.fori_loop(1, OWNERS, begin, 0)
    came[tile] = out[tile]
    lax.fori_loop(1, OWNERS, finish, 0)


def request_kernel(owner, local, anchor, frac_x, frac_y, label, codes, slot_out, out, came, send_sem, recv_sem):
    tile, rep = position()
    barrier = pltpu.get_barrier_semaphore()
    greet_tile(barrier, tile, rep)
    message, slot = request_rows(owner[...], local[...], anchor[...], frac_x[...], frac_y[...], label[...])
    slot_out[...] = slot
    for k in range(OWNERS):
        out[k] = message[k:k + 1, :]
    pl.semaphore_wait(barrier, OWNERS - 1)
    exchange(tile, rep, out, came, send_sem, recv_sem)
    arrived = jnp.concatenate([came[k] for k in range(OWNERS)], axis=0)
    pair = jnp.concatenate([arrived, pltpu.roll(arrived, 128 - 12, 1)], axis=0)
    codes[...] = pair.T


def request(rows):
    return pl.pallas_call(
        request_kernel,
        out_shape=(jax.ShapeDtypeStruct((128, 128), jnp.float32), jax.ShapeDtypeStruct((1, FIXES), jnp.float32)),
        in_specs=[VMEM] * 6,
        out_specs=(VMEM, VMEM),
        scratch_shapes=[
            pltpu.VMEM((OWNERS, 1, 128), jnp.float32),
            pltpu.VMEM((OWNERS, 1, 128), jnp.float32),
            pltpu.SemaphoreType.DMA((OWNERS,)),
            pltpu.SemaphoreType.DMA((OWNERS,)),
        ],
        compiler_params=pltpu.CompilerParams(collective_id=0, has_side_effects=True, vmem_limit_bytes=LIMIT),
    )(*rows)


def swap_rows_and_tiles(raster, turned):
    group = iota((LAYERS, 128), 1) // 16
    for half in range(2):
        for part in range(2):
            held = [raster[8 * part + t, :, half * 128:(half + 1) * 128].astype(jnp.float32) for t in range(8)]
            for step in (1, 2, 4):
                upper = (group // step) % 2 == 1
                for t in range(8):
                    if t & step == 0:
                        a, b = held[t], held[t | step]
                        held[t] = jnp.where(upper, pltpu.roll(b, 16 * step, 1), a)
                        held[t | step] = jnp.where(upper, b, pltpu.roll(a, 128 - 16 * step, 1))
            for r in range(8):
                row = 8 * half + r
                turned[row * 64:(row + 1) * 64, part * 128:(part + 1) * 128] = held[r].astype(jnp.bfloat16)


def terms_kernel(codes, raster, beta, packed, rows_out, turned, scaled, resid):
    swap_rows_and_tiles(raster, turned)
    beta_parts = stacked_thirds(beta[...])

    def block(at):
        def field(f):
            return jnp.concatenate([codes[pl.ds(f * SLOTS + 2 * at, 1), :], codes[pl.ds(f * SLOTS + 2 * at + 1, 1), :]], axis=1)

        local, anchor, frac_x, frac_y, mark = [field(f) for f in range(5)]
        row = jnp.floor((anchor + 0.5) * (1.0 / 15.0))
        cell = local * 16.0 + (anchor - 15.0 * row)
        lane = iota((256, 256), 0).astype(jnp.float32)
        weight_x = jnp.where(lane == cell, 256.0 - frac_x, 0.0) + jnp.where(lane == cell + 1.0, frac_x, 0.0)
        along = dot(turned[...], weight_x.astype(jnp.bfloat16))
        values = None
        for r in range(16):
            weight_y = jnp.where(row == float(r), 256.0 - frac_y, 0.0) + jnp.where(row == float(r - 1), frac_y, 0.0)
            term = weight_y * along[r * 64:(r + 1) * 64]
            values = term if values is None else values + term
        values = values * (1.0 / 65536.0)
        spread = jnp.broadcast_to(values[:, None, :], (LAYERS, SPLINES, 256))
        knots = 0.5 * (iota((LAYERS, SPLINES, 256), 1).astype(jnp.float32) - 0.5 * (SPLINES - 1))
        bump = jnp.maximum(1.0 - jnp.abs(spread - knots) * (1.0 / 0.75), 0.0)
        rows = (bump * bump * bump).reshape(BASIS, 256).astype(jnp.bfloat16)
        lanes = pl.ds(pl.multiple_of(at * 256, 256), 256)
        rows_out[:, lanes] = rows
        eta = jnp.sum(dot(beta_parts, rows), axis=0, keepdims=True)
        live = (mark > 0.5).astype(jnp.float32)
        outcome = mark - 1.0
        prob = 1.0 / (1.0 + jnp.exp(-eta))
        weight = prob * (1.0 - prob) * live
        scaled[:, lanes] = (jnp.sqrt(weight) * rows.astype(jnp.float32)).astype(jnp.bfloat16)
        resid[:, lanes] = stacked_thirds(weight * eta + (outcome - prob) * live)

    pl.loop(0, 6)(block)
    target = jnp.sum(dot(resid[...], rows_out[...], NT), axis=0, keepdims=True)
    for chunk in range(32):
        packed[chunk, 40:48, :] = jnp.zeros((8, 128), jnp.float32)
    for part in range(4):
        packed[part, 40:41, :] = target[:, part * 128:(part + 1) * 128]
    tile = 0
    for i in range(4):
        panel = dot(scaled[i * 128:(i + 1) * 128, :], scaled[i * 128:, :], NT)
        for j in range(i, 4):
            for r in range(16):
                packed[tile // 5, tile % 5 * 8:tile % 5 * 8 + 8, :] = panel[r * 8:r * 8 + 8, (j - i) * 128:(j - i + 1) * 128]
                tile += 1


def terms(codes, raster, beta):
    return pl.pallas_call(
        terms_kernel,
        out_shape=(
            jax.ShapeDtypeStruct((32, ROWS, 128), jnp.float32),
            jax.ShapeDtypeStruct((BASIS, OWNERS * SLOTS), jnp.bfloat16),
        ),
        in_specs=[VMEM] * 3,
        out_specs=(VMEM, VMEM),
        scratch_shapes=[
            pltpu.VMEM((1024, 256), jnp.bfloat16),
            pltpu.VMEM((BASIS, OWNERS * SLOTS), jnp.bfloat16),
            pltpu.VMEM((16, OWNERS * SLOTS), jnp.bfloat16),
        ],
        compiler_params=pltpu.CompilerParams(vmem_limit_bytes=LIMIT),
    )(codes, raster, beta)


def total_kernel(packed, out, mate_in, paired, plane_in, deep_out, deep_in, part, deep_back, whole, result,
                 s_mate, r_mate, s_plane, r_plane, s_deep, r_deep, s_back, r_back, s_wide, r_wide, s_last, r_last):
    tile, rep = position()
    x, z = lax.div(tile, DEEP), lax.rem(tile, DEEP)
    y, core = lax.div(rep, 2), lax.rem(rep, 2)
    me = x * 4 + y
    mate = (tile, rep + 1 - 2 * core)

    def chip(p):
        return (lax.div(p, 4) * DEEP + z, lax.rem(p, 4) * 2 + core)

    def level(k):
        return (x * DEEP + k, rep)

    barrier = pltpu.get_barrier_semaphore()
    pl.semaphore_signal(barrier, inc=1, device_id=mate, device_id_type=MESH)

    def greet(step, _):
        pl.semaphore_signal(barrier, inc=1, device_id=chip(lax.rem(me + step, PLANE)), device_id_type=MESH)
        pl.semaphore_signal(barrier, inc=1, device_id=level(lax.rem(z + step, DEEP)), device_id_type=MESH)
        return 0

    lax.fori_loop(1, PLANE, greet, 0)
    pl.semaphore_wait(barrier, 1 + (PLANE - 1) + (DEEP - 1))

    def remote(src, dst, send, recv, device):
        return pltpu.make_async_remote_copy(
            src_ref=src, dst_ref=dst, send_sem=send, recv_sem=recv, device_id=device, device_id_type=MESH)

    def to_mate(p):
        return remote(packed.at[(1 - core) * PLANE + p], mate_in.at[p], s_mate.at[p], r_mate.at[p], mate)

    def to_plane(p, slot):
        return remote(paired.at[p], plane_in.at[slot], s_plane.at[p], r_plane.at[slot], chip(p))

    def to_level(k, slot):
        return remote(deep_out.at[k], deep_in.at[slot], s_deep.at[k], r_deep.at[slot], level(k))

    def back_level(k, slot):
        return remote(part, deep_back.at[slot], s_back.at[k], r_back.at[slot], level(k))

    def back_plane(p, slot):
        return remote(whole, result.at[core * PLANE + slot], s_wide.at[p], r_wide.at[slot], chip(p))

    def back_mate(p, half):
        at = half * PLANE + p
        return remote(result.at[at], result.at[at], s_last.at[p], r_last.at[p], mate)

    def each(count, mine, body, first=1, last=None):
        def step(k, _):
            body(lax.rem(mine + k, count))
            return 0

        lax.fori_loop(first, count if last is None else last, step, 0)

    each(PLANE, me, lambda p: to_mate(p).start(), 1, PLANE + 1)

    def pair_sum(p):
        to_mate(p).wait_recv()
        paired[p] = packed[core * PLANE + p] + mate_in[p]

    def pair_and_send(p):
        pair_sum(p)
        to_plane(p, me).start()

    each(PLANE, me, pair_and_send)
    pair_sum(me)

    def gather_plane(k, total):
        p = lax.rem(me + k, PLANE)
        to_plane(p, p).wait_recv()
        return total + plane_in[p]

    total = lax.fori_loop(1, PLANE, gather_plane, paired[me])
    for k in range(DEEP):
        deep_out[k] = total[3 * k:3 * k + 3, :]
    each(DEEP, z, lambda k: to_level(k, z).start())

    def gather_level(step, total):
        k = lax.rem(z + step, DEEP)
        to_level(k, k).wait_recv()
        return total + deep_in[k]

    part[...] = lax.fori_loop(1, DEEP, gather_level, deep_out[z])

    each(DEEP, z, lambda k: back_level(k, z).start())
    deep_back[z] = part[...]
    each(DEEP, z, lambda k: back_level(k, k).wait_recv())
    for k in range(DEEP):
        whole[3 * k:3 * k + 3, :] = deep_back[k]
    each(PLANE, me, lambda p: back_plane(p, me).start())
    result[core * PLANE + me] = whole[...]
    back_mate(me, core).start()

    def forward(p):
        back_plane(p, p).wait_recv()
        back_mate(p, core).start()

    each(PLANE, me, forward)
    each(PLANE, me, lambda p: back_mate(p, 1 - core).wait_recv(), 0)

    each(PLANE, me, lambda p: to_mate(p).wait_send(), 0)
    each(PLANE, me, lambda p: to_plane(p, me).wait_send())
    each(DEEP, z, lambda k: to_level(k, z).wait_send())
    each(DEEP, z, lambda k: back_level(k, z).wait_send())
    each(PLANE, me, lambda p: back_plane(p, me).wait_send())
    each(PLANE, me, lambda p: back_mate(p, core).wait_send(), 0)

    def write(k, _):
        out[k] = result[k]
        return 0

    lax.fori_loop(0, 32, write, 0)


def total(packed):
    dma = pltpu.SemaphoreType.DMA((PLANE,))
    f32 = jnp.float32
    return pl.pallas_call(
        total_kernel,
        out_shape=jax.ShapeDtypeStruct((32, ROWS, 128), f32),
        in_specs=[VMEM],
        out_specs=VMEM,
        scratch_shapes=[
            pltpu.VMEM((PLANE, ROWS, 128), f32),
            pltpu.VMEM((PLANE, ROWS, 128), f32),
            pltpu.VMEM((PLANE, ROWS, 128), f32),
            pltpu.VMEM((DEEP, 3, 128), f32),
            pltpu.VMEM((DEEP, 3, 128), f32),
            pltpu.VMEM((3, 128), f32),
            pltpu.VMEM((DEEP, 3, 128), f32),
            pltpu.VMEM((ROWS, 128), f32),
            pltpu.VMEM((32, ROWS, 128), f32),
        ] + [dma] * 12,
        compiler_params=pltpu.CompilerParams(collective_id=1, has_side_effects=True, vmem_limit_bytes=LIMIT),
    )(packed)


def reciprocal(x):
    guess = pl.reciprocal(x, approx=True)
    guess = guess * (2.0 - x * guess)
    return guess * (2.0 - x * guess)


def invert(tiles):
    tiles = list(tiles)
    lane = iota((8, 128), 1)
    row = iota((8, 128), 0)

    def take(tile, m):
        return jnp.broadcast_to(tile[m:m + 1, :], (8, 128))

    for b in range(16):
        inside = (lane // 8) == b
        columns = [jnp.broadcast_to(tiles[b][:, 8 * b + m:8 * b + m + 1], (8, 128)) for m in range(8)]
        lead = jnp.where(inside, jnp.where(lane - 8 * b == row, 1.0, 0.0), tiles[b])
        for m in range(0, 8, 2):
            p, q, r = take(columns[m], m), take(columns[m + 1], m), take(columns[m + 1], m + 1)
            scale = reciprocal(p * r - q * q)
            is_first, is_second = row == m, row == m + 1

            def sweep(tile):
                first, second = take(tile, m), take(tile, m + 1)
                first, second = (r * first - q * second) * scale, (p * second - q * first) * scale
                rest = tile - columns[m] * first - columns[m + 1] * second
                return jnp.where(is_first, first, jnp.where(is_second, second, rest))

            later = [sweep(columns[k]) for k in range(m + 2, 8)]
            lead = sweep(lead)
            columns = columns[:m + 2] + later
        taken = [take(lead, m) for m in range(8)]
        for i in range(16):
            if i != b:
                source = tiles[i]
                update = jnp.where(inside, 0.0, source)
                for m in range(8):
                    update = update - jnp.broadcast_to(source[:, 8 * b + m:8 * b + m + 1], (8, 128)) * taken[m]
                tiles[i] = update
        tiles[b] = lead
    return tiles


def second_difference():
    i, j = iota((8, 128), 0), iota((8, 128), 1) % 8
    inner = jnp.zeros((8, 128), jnp.float32)

    def entry(at, r):
        return jnp.where(at == r, 1.0, 0.0) - jnp.where(at == r + 1, 2.0, 0.0) + jnp.where(at == r + 2, 1.0, 0.0)

    for r in range(SPLINES - 2):
        inner = inner + entry(i, r) * entry(j, r)
    return inner


def solve_kernel(sums, smooth, beta_new, system, scaled, right):
    count = 1.0 / (FIXES * 512.0)
    lane, row = iota((8, 128), 1), iota((8, 128), 0)
    inner = second_difference()
    tile = 0
    for i, j in BLOCKS:
        for r in range(16):
            value = sums[tile // 5, tile % 5 * 8:tile % 5 * 8 + 8, :] * count
            if i == j:
                value = value + jnp.where(lane // 8 == r, smooth[16 * i + r] * inner, 0.0)
                value = value + jnp.where(lane == row + 8 * r, RIDGE, 0.0)
            system[i, r * 8:r * 8 + 8, j * 128:(j + 1) * 128] = value
            tile += 1
    for part in range(4):
        right[part] = sums[part, 40:41, :] * count

    inverse = []
    done = []
    for k in range(4):
        tiles = invert([system[k, r * 8:r * 8 + 8, k * 128:(k + 1) * 128] for r in range(16)])
        inverse = jnp.concatenate(tiles, axis=0)
        mine = dot(jnp.broadcast_to(right[k], (8, 128)), inverse, precision=HIGHEST)
        done.append(mine)
        if k < 3:
            after = system[k, :, (k + 1) * 128:]
            spread = dot(inverse, after, precision=HIGHEST)
            scaled[k, :, (k + 1) * 128:] = spread
            shift = dot(mine, after, precision=HIGHEST)
            for i in range(k + 1, 4):
                right[i] = right[i] - shift[0:1, (i - k - 1) * 128:(i - k) * 128]
                lead = system[k, :, i * 128:(i + 1) * 128]
                change = dot(lead.T, spread[:, (i - k - 1) * 128:], precision=HIGHEST)
                system[i, :, i * 128:] = system[i, :, i * 128:] - change
    found = [None, None, None, done[3]]
    for k in (2, 1, 0):
        later = jnp.concatenate(found[k + 1:], axis=1)
        found[k] = done[k] - dot(later, scaled[k, :, (k + 1) * 128:], NT, precision=HIGHEST)
    for k in range(4):
        beta_new[:, k * 128:(k + 1) * 128] = found[k][0:1, :]


def solve(sums, smooth):
    return pl.pallas_call(
        solve_kernel,
        out_shape=jax.ShapeDtypeStruct((1, BASIS), jnp.float32),
        in_specs=[VMEM, SMEM],
        out_specs=VMEM,
        scratch_shapes=[
            pltpu.VMEM((4, 128, BASIS), jnp.float32),
            pltpu.VMEM((4, 128, BASIS), jnp.float32),
            pltpu.VMEM((4, 1, 128), jnp.float32),
        ],
        compiler_params=pltpu.CompilerParams(vmem_limit_bytes=LIMIT),
    )(sums, smooth)


def predict_rows(rows, beta_new):
    eta = jnp.sum(dot(stacked_thirds(beta_new), rows), axis=0, keepdims=True)
    lines = [eta[:, b * 128:(b + 1) * 128] for b in range(12)]
    turned = jnp.concatenate(lines + [jnp.zeros((116, 128), jnp.float32)], axis=0).T
    lane = iota((OWNERS, 128), 1)
    return jnp.where(lane < 12, turned[:OWNERS], pltpu.roll(turned[OWNERS:], 12, 1))


def unpack_rows(arrived, owner, slot):
    named = (iota((OWNERS, FIXES), 0) == owner).astype(jnp.float32).astype(jnp.bfloat16)
    high, mid, low = thirds(arrived.T)
    spread = dot(high, named) + dot(mid, named) + dot(low, named)
    at = iota((SLOTS, FIXES), 0).astype(jnp.float32) == slot
    return jnp.sum(jnp.where(at, spread[:SLOTS], 0.0), axis=0, keepdims=True)


def predict_kernel(rows, beta_new, owner, slot, eta_new, out, came, send_sem, recv_sem):
    tile, rep = position()
    barrier = pltpu.get_barrier_semaphore()
    greet_tile(barrier, tile, rep)
    message = predict_rows(rows[...], beta_new[...])
    for k in range(OWNERS):
        out[k] = message[k:k + 1, :]
    pl.semaphore_wait(barrier, OWNERS - 1)
    exchange(tile, rep, out, came, send_sem, recv_sem)
    arrived = jnp.concatenate([came[k] for k in range(OWNERS)], axis=0)
    eta_new[...] = unpack_rows(arrived, owner[...], slot[...])


def predict(rows, beta_new, owner, slot):
    return pl.pallas_call(
        predict_kernel,
        out_shape=jax.ShapeDtypeStruct((1, FIXES), jnp.float32),
        in_specs=[VMEM] * 4,
        out_specs=VMEM,
        scratch_shapes=[
            pltpu.VMEM((OWNERS, 1, 128), jnp.float32),
            pltpu.VMEM((OWNERS, 1, 128), jnp.float32),
            pltpu.SemaphoreType.DMA((OWNERS,)),
            pltpu.SemaphoreType.DMA((OWNERS,)),
        ],
        compiler_params=pltpu.CompilerParams(collective_id=2, has_side_effects=True, vmem_limit_bytes=LIMIT),
    )(rows, beta_new, owner, slot)


def shards(owner, tile_local, anchor, frac_x, frac_y, label, raster, beta, smooth):
    line = lambda array: array.reshape(1, FIXES)
    owner = line(owner)
    codes, slot = request([owner] + [line(a) for a in (tile_local, anchor, frac_x, frac_y, label)])
    packed, rows = terms(codes, raster, beta.reshape(1, BASIS))
    beta_new = solve(total(packed), smooth)
    eta_new = predict(rows, beta_new, owner, slot)
    return beta_new.reshape(BASIS), eta_new.reshape(FIXES)


def solution(mesh):
    fixes = P(("tile", "rep"))
    placed = (P(("tile", "rep"), None), fixes, fixes, fixes, fixes, fixes, P("tile", None, None), P(), P())
    return jax.shard_map(shards, mesh=mesh, in_specs=placed, out_specs=(P(), fixes), check_vma=False)
```

time: 827 us -> 130 us (0.16)
  waiting for transfers between devices: 408 us -> 0 us
  other arithmetic: 136 us -> 0 us
  Pallas kernels: 0 us -> 122 us
  blocking collectives: 107 us -> 0 us
  local copies, waits for them, and re-layouts: 99.6 us -> 7.07 us
  starting transfers between devices: 38.9 us -> 0 us
  between operations: 17.5 us -> 0.7 us
  matrix products: 12.7 us -> 0 us
    psum x1 -> x0, waiting for transfers between devices: 359 us -> none  [shards(): gram, target = lax.psum((gram, target), ('tile', 'rep'))]
    pallas_call x0 -> x5, Pallas kernels: none -> 122 us  [the longest x1 44.4 us: total(): pl.pallas_call(total_kernel, out_shape=jax.ShapeDtypeStruct((32, ROWS, 12...]
    another operation x22 -> x0, other arithmetic: 121 us -> none  [the longest x15 79.4 us: solve_step(): factor = jnp.linalg.cholesky(system)]
    psum x1 -> x0, blocking collectives: 107 us -> none  [shards(): gram, target = lax.psum((gram, target), ('tile', 'rep'))]
    all_to_all x2 -> x0, waiting for transfers between devices: 48.2 us -> none  [the longest x1 34.9 us: shards(): lax.all_to_all(expand(values), 'tile', split_axis=0, concat_axis=0, tiled...]
    gather x5 -> x0, local copies, waits for them, and re-layouts: 37.8 us -> none  [the longest x1 8.47 us: interpolate(): upper_right = raster[tiles, :, corner + 17].astype(jnp.float32)]
    all_to_all x2 -> x0, starting transfers between devices: 26.7 us -> none  [the longest x1 19.1 us: shards(): lax.all_to_all(codes, 'tile', split_axis=1, concat_axis=1, tiled=True)]
    scatter x2 -> x0, local copies, waits for them, and re-layouts: 25.2 us -> none  [pack_fields(): return empty.at[:, owners, slots].set(stacked)]
  transfers between devices with their start and end apart: 3 -> 0, of which waited for: 3 -> 0; matrix products, arithmetic and copies ran while one was open for 3% -> 0% of each run, Pallas kernels for 0% -> 0%
where the time goes in v1:
time: 130 us; the launch traced here: 129 us
  Pallas kernels  122 us (94%)
  local copies, waits for them, and re-layouts  7.07 us (5%)
    pallas_call x1, Pallas kernels, total(): pl.pallas_call(total_kernel, out_shape=jax.ShapeDtypeStruct((32, ROWS, 12...  44.4 us
    pallas_call x1, Pallas kernels, solve(): pl.pallas_call(solve_kernel, out_shape=jax.ShapeDtypeStruct((1, BASIS), j...  28.1 us
    pallas_call x1, Pallas kernels, request(): pl.pallas_call(request_kernel, out_shape=(jax.ShapeDtypeStruct((128, 128)...  24.9 us
    pallas_call x1, Pallas kernels, predict(): pl.pallas_call(predict_kernel, out_shape=jax.ShapeDtypeStruct((1, FIXES),...  17.3 us
    unnamed x21, local copies, waits for them, and re-layouts  7.07 us
    pallas_call x1, Pallas kernels, terms(): pl.pallas_call(terms_kernel, out_shape=(jax.ShapeDtypeStruct((32, ROWS, 1...  6.99 us

profile of v1, /device:TPU:1, one launch (start us, length us, event | category | flops | bytes accessed | tf_op | source)
XLA Modules:
  0.0 129.4 jit_solution(10458713629974977364)
XLA Ops:
  0.6 0.0 copy-start.9
  0.6 0.0 copy-start.2
  0.7 0.7 copy-done.2
  1.3 0.0 copy-start.4
  1.3 0.7 copy-done.4
  2.0 0.0 copy-start.5
  2.0 0.7 copy-done.5
  2.7 0.0 copy-start.6
  2.7 0.7 copy-done.6
  3.4 0.0 copy-start.7
  3.4 0.7 copy-done.7
  4.1 0.0 copy-start.8
  4.1 0.7 copy-done.8
  4.7 24.9 %shard_map.104 = (f32[128,128]{1,0:T(8,128)S(1)}, f32[1,512]{1,0:T(1,128)S(1)}) custom-call(s32[1,512]{1,0:T(1,128)S(1)} %bitcast.11, s32[1,512]{1,0:T(1,128)S(1)} %bitcast.14, s32[1,512]{1,0:T(1,128)S(1)} %bitcast.15, s32[1,512]{1,0:T(1,128)S(1)} %bitcast.16, s32[1,512]{1,0:T(1,128)S(1)} %bitcast.17, s32[1,512]{1,0:T(1,128)S(1)} %bitcast.18), custom_call_target="tpu_custom_call" | custom-call | tf_op jit(solution)/shard_map/pallas_call | solution.py:116
  29.6 0.0 copy-start
  29.6 1.0 copy-done
  30.7 0.0 copy-start.3
  30.7 0.7 copy-done.3
  31.3 7.0 %shard_map.105 = (f32[32,48,128]{2,1,0:T(8,128)S(1)}, bf16[512,1536]{1,0:T(8,128)(2,1)S(1)}) custom-call(f32[128,128]{1,0:T(8,128)S(1)} %get-tuple-element.6.codes, bf16[16,64,256]{2,1,0:T(8,128)(2,1)S(1)} %copy-done, f32[1,512]{1,0:T(1,128)S(1)} %bitcast.13), custom_call_target="tpu_custom_call" | custom-call | tf_op jit(solution)/shard_map/pallas_call | solution.py:198
  38.3 44.4 %shard_map.106.sums = f32[32,48,128]{2,1,0:T(8,128)S(1)} custom-call(f32[32,48,128]{2,1,0:T(8,128)S(1)} %get-tuple-element.7.packed), custom_call_target="tpu_custom_call" | custom-call | tf_op jit(solution)/shard_map/pallas_call | solution.py:333
  82.8 0.0 copy-done.9
  82.8 28.1 %shard_map.107.beta_new = f32[1,512]{1,0:T(1,128)} custom-call(f32[32,48,128]{2,1,0:T(8,128)S(1)} %shard_map.106.sums, f32[64]{0:T(128)S(1)} %copy-done.9), custom_call_target="tpu_custom_call" | custom-call | tf_op jit(solution)/shard_map/pallas_call | solution.py:451
  110.8 0.0 copy-start.1
  110.8 0.7 copy-done.1
  111.5 17.3 %shard_map.108 = f32[1,512]{1,0:T(1,128)S(1)} custom-call(bf16[512,1536]{1,0:T(8,128)(2,1)S(1)} %get-tuple-element.8.rows, f32[1,512]{1,0:T(1,128)S(1)} %copy-done.1, s32[1,512]{1,0:T(1,128)S(1)} %bitcast.12, f32[1,512]{1,0:T(1,128)S(1)} %get-tuple-element.9.slot), custom_call_target="tpu_custom_call" | custom-call | tf_op jit(solution)/shard_map/pallas_call | solution.py:495
  128.9 0.6 copy.12
Async XLA Ops:
  0.6 82.1 %copy-start.9 = (f32[64]{0:T(128)S(1)}, f32[64]{0:T(128)}, u32[]{:S(2)}) copy-start(f32[64]{0:T(128)} %smooth.1) | copy-start | bytes 772
  0.6 0.7 copy-start.2
  1.3 0.7 copy-start.4
  2.0 0.7 copy-start.5
  2.7 0.7 copy-start.6
  3.4 0.7 copy-start.7
  4.1 0.7 copy-start.8
  29.6 1.0 copy-start
  30.7 0.7 copy-start.3
  110.8 0.7 copy-start.1

commit v2 on v1

--- a/solution.py
+++ b/solution.py
@@ -14,14 +14,17 @@
 FIXES = 512
 SLOTS = 24
 OWNERS = 64
-PLANE = 16
 DEEP = 16
-ROWS = 48
+GROUP = 32
+LEVELS = 8
+ROWS = 24
+GRAM_TILES = 160
+TARGET_ROW = GRAM_TILES % 3 * 8
 MESH = pl.DeviceIdType.MESH
 HIGHEST = lax.Precision.HIGHEST
 VMEM = pl.BlockSpec(memory_space=pltpu.VMEM)
 SMEM = pl.BlockSpec(memory_space=pltpu.SMEM)
-LIMIT = 48 * 1024 * 1024
+LIMIT = 62 * 1024 * 1024
 BLOCKS = [(i, j) for i in range(4) for j in range(i, 4)]
 NT = (((1,), (1,)), ((), ()))
 TN = (((0,), (0,)), ((), ()))
@@ -95,37 +98,6 @@
     lax.fori_loop(1, OWNERS, begin, 0)
     came[tile] = out[tile]
     lax.fori_loop(1, OWNERS, finish, 0)
-
-
-def request_kernel(owner, local, anchor, frac_x, frac_y, label, codes, slot_out, out, came, send_sem, recv_sem):
-    tile, rep = position()
-    barrier = pltpu.get_barrier_semaphore()
-    greet_tile(barrier, tile, rep)
-    message, slot = request_rows(owner[...], local[...], anchor[...], frac_x[...], frac_y[...], label[...])
-    slot_out[...] = slot
-    for k in range(OWNERS):
-        out[k] = message[k:k + 1, :]
-    pl.semaphore_wait(barrier, OWNERS - 1)
-    exchange(tile, rep, out, came, send_sem, recv_sem)
-    arrived = jnp.concatenate([came[k] for k in range(OWNERS)], axis=0)
-    pair = jnp.concatenate([arrived, pltpu.roll(arrived, 128 - 12, 1)], axis=0)
-    codes[...] = pair.T
-
-
-def request(rows):
-    return pl.pallas_call(
-        request_kernel,
-        out_shape=(jax.ShapeDtypeStruct((128, 128), jnp.float32), jax.ShapeDtypeStruct((1, FIXES), jnp.float32)),
-        in_specs=[VMEM] * 6,
-        out_specs=(VMEM, VMEM),
-        scratch_shapes=[
-            pltpu.VMEM((OWNERS, 1, 128), jnp.float32),
-            pltpu.VMEM((OWNERS, 1, 128), jnp.float32),
-            pltpu.SemaphoreType.DMA((OWNERS,)),
-            pltpu.SemaphoreType.DMA((OWNERS,)),
-        ],
-        compiler_params=pltpu.CompilerParams(collective_id=0, has_side_effects=True, vmem_limit_bytes=LIMIT),
-    )(*rows)
 
 
 def swap_rows_and_tiles(raster, turned):
@@ -145,8 +117,7 @@
                 turned[row * 64:(row + 1) * 64, part * 128:(part + 1) * 128] = held[r].astype(jnp.bfloat16)
 
 
-def terms_kernel(codes, raster, beta, packed, rows_out, turned, scaled, resid):
-    swap_rows_and_tiles(raster, turned)
+def form_terms(codes, beta, packed, rows_out, turned, scaled, resid):
     beta_parts = stacked_thirds(beta[...])
 
     def block(at):
@@ -181,173 +152,193 @@
 
     pl.loop(0, 6)(block)
     target = jnp.sum(dot(resid[...], rows_out[...], NT), axis=0, keepdims=True)
-    for chunk in range(32):
-        packed[chunk, 40:48, :] = jnp.zeros((8, 128), jnp.float32)
+    for spare in range(GRAM_TILES, 2 * GROUP * 3):
+        packed[spare // 3, spare % 3 * 8:spare % 3 * 8 + 8, :] = jnp.zeros((8, 128), jnp.float32)
     for part in range(4):
-        packed[part, 40:41, :] = target[:, part * 128:(part + 1) * 128]
+        packed[GRAM_TILES // 3, TARGET_ROW + part:TARGET_ROW + part + 1, :] = target[:, part * 128:(part + 1) * 128]
     tile = 0
     for i in range(4):
         panel = dot(scaled[i * 128:(i + 1) * 128, :], scaled[i * 128:, :], NT)
         for j in range(i, 4):
             for r in range(16):
-                packed[tile // 5, tile % 5 * 8:tile % 5 * 8 + 8, :] = panel[r * 8:r * 8 + 8, (j - i) * 128:(j - i + 1) * 128]
+                packed[tile // 3, tile % 3 * 8:tile % 3 * 8 + 8, :] = panel[r * 8:r * 8 + 8, (j - i) * 128:(j - i + 1) * 128]
                 tile += 1
 
 
-def terms(codes, raster, beta):
-    return pl.pallas_call(
-        terms_kernel,
-        out_shape=(
-            jax.ShapeDtypeStruct((32, ROWS, 128), jnp.float32),
-            jax.ShapeDtypeStruct((BASIS, OWNERS * SLOTS), jnp.bfloat16),
-        ),
-        in_specs=[VMEM] * 3,
-        out_specs=(VMEM, VMEM),
-        scratch_shapes=[
-            pltpu.VMEM((1024, 256), jnp.bfloat16),
-            pltpu.VMEM((BASIS, OWNERS * SLOTS), jnp.bfloat16),
-            pltpu.VMEM((16, OWNERS * SLOTS), jnp.bfloat16),
-        ],
-        compiler_params=pltpu.CompilerParams(vmem_limit_bytes=LIMIT),
-    )(codes, raster, beta)
-
-
-def total_kernel(packed, out, mate_in, paired, plane_in, deep_out, deep_in, part, deep_back, whole, result,
-                 s_mate, r_mate, s_plane, r_plane, s_deep, r_deep, s_back, r_back, s_wide, r_wide, s_last, r_last):
+def add_up(place, packed, mate_in, paired, group_in, mine, level_in, whole, result, sems):
+    s_mate, r_mate, s_group, r_group, s_level, r_level, s_wide, r_wide, s_last, r_last = sems
+    me, core, pair, mate, chip, level = place
+
+    def remote(src, dst, send, recv, device):
+        return pltpu.make_async_remote_copy(
+            src_ref=src, dst_ref=dst, send_sem=send, recv_sem=recv, device_id=device, device_id_type=MESH)
+
+    def to_mate(p):
+        return remote(packed.at[(1 - core) * GROUP + p], mate_in.at[p], s_mate.at[p], r_mate.at[p], mate)
+
+    def to_chip(p, slot):
+        return remote(paired.at[p], group_in.at[slot], s_group.at[p], r_group.at[slot], chip(p))
+
+    def to_level(k, slot):
+        return remote(mine, level_in.at[slot], s_level.at[k], r_level.at[slot], level(k))
+
+    def back_chip(p, slot):
+        return remote(whole, result.at[core * GROUP + slot], s_wide.at[p], r_wide.at[slot], chip(p))
+
+    def back_mate(p, half):
+        at = half * GROUP + p
+        return remote(result.at[at], result.at[at], s_last.at[p], r_last.at[p], mate)
+
+    def each(body, first=1, last=GROUP):
+        def step(k, _):
+            body(lax.rem(me + k, GROUP))
+            return 0
+
+        lax.fori_loop(first, last, step, 0)
+
+    each(lambda p: to_mate(p).start(), 1, GROUP + 1)
+
+    def pair_sum(p):
+        to_mate(p).wait_recv()
+        paired[p] = packed[core * GROUP + p] + mate_in[p]
+
+    def pair_and_send(p):
+        pair_sum(p)
+        to_chip(p, me).start()
+
+    each(pair_and_send)
+    pair_sum(me)
+
+    def gather(k, total):
+        p = lax.rem(me + k, GROUP)
+        to_chip(p, p).wait_recv()
+        return total + group_in[p]
+
+    mine[...] = lax.fori_loop(1, GROUP, gather, paired[me])
+    others = [lax.rem(pair + step, LEVELS) for step in (4, 3, 5, 2, 6, 1, 7)]
+    for k in others:
+        to_level(k, pair).start()
+    level_in[pair] = mine[...]
+    for k in others:
+        to_level(k, k).wait_recv()
+    total = level_in[0]
+    for k in range(1, LEVELS):
+        total = total + level_in[k]
+    whole[...] = total
+
+    each(lambda p: back_chip(p, me).start())
+    result[core * GROUP + me] = total
+    back_mate(me, core).start()
+
+    def forward(p):
+        back_chip(p, p).wait_recv()
+        back_mate(p, core).start()
+
+    each(forward)
+    each(lambda p: back_mate(p, 1 - core).wait_recv(), 0)
+
+    each(lambda p: to_mate(p).wait_send(), 0)
+    each(lambda p: to_chip(p, me).wait_send())
+    for k in others:
+        to_level(k, pair).wait_send()
+    each(lambda p: back_chip(p, me).wait_send())
+    each(lambda p: back_mate(p, core).wait_send(), 0)
+
+
+def sums_kernel(owner, local, anchor, frac_x, frac_y, label, raster, beta, out, rows_out, slot_out,
+                lines, raster_in, beta_in, out_codes, came, codes, turned, scaled, resid,
+                packed, mate_in, paired, group_in, mine, level_in, whole, result, loads, send_sem, recv_sem, *sems):
     tile, rep = position()
     x, z = lax.div(tile, DEEP), lax.rem(tile, DEEP)
     y, core = lax.div(rep, 2), lax.rem(rep, 2)
-    me = x * 4 + y
+    pair, low = lax.div(z, 2), lax.rem(z, 2)
+    me = (x * 4 + y) * 2 + low
     mate = (tile, rep + 1 - 2 * core)
 
     def chip(p):
-        return (lax.div(p, 4) * DEEP + z, lax.rem(p, 4) * 2 + core)
+        return (lax.div(p, 8) * DEEP + pair * 2 + lax.rem(p, 2), lax.rem(lax.div(p, 2), 4) * 2 + core)
 
     def level(k):
-        return (x * DEEP + k, rep)
+        return (x * DEEP + k * 2 + low, rep)
 
     barrier = pltpu.get_barrier_semaphore()
+    greet_tile(barrier, tile, rep)
     pl.semaphore_signal(barrier, inc=1, device_id=mate, device_id_type=MESH)
 
     def greet(step, _):
-        pl.semaphore_signal(barrier, inc=1, device_id=chip(lax.rem(me + step, PLANE)), device_id_type=MESH)
-        pl.semaphore_signal(barrier, inc=1, device_id=level(lax.rem(z + step, DEEP)), device_id_type=MESH)
+        other_y = lax.rem(y + 1 + lax.rem(step, 3), 4)
+        rest = lax.div(step, 3)
+        device = (lax.div(rest, 2) * DEEP + pair * 2 + lax.rem(rest, 2), other_y * 2 + core)
+        pl.semaphore_signal(barrier, inc=1, device_id=device, device_id_type=MESH)
         return 0
 
-    lax.fori_loop(1, PLANE, greet, 0)
-    pl.semaphore_wait(barrier, 1 + (PLANE - 1) + (DEEP - 1))
-
-    def remote(src, dst, send, recv, device):
-        return pltpu.make_async_remote_copy(
-            src_ref=src, dst_ref=dst, send_sem=send, recv_sem=recv, device_id=device, device_id_type=MESH)
-
-    def to_mate(p):
-        return remote(packed.at[(1 - core) * PLANE + p], mate_in.at[p], s_mate.at[p], r_mate.at[p], mate)
-
-    def to_plane(p, slot):
-        return remote(paired.at[p], plane_in.at[slot], s_plane.at[p], r_plane.at[slot], chip(p))
-
-    def to_level(k, slot):
-        return remote(deep_out.at[k], deep_in.at[slot], s_deep.at[k], r_deep.at[slot], level(k))
-
-    def back_level(k, slot):
-        return remote(part, deep_back.at[slot], s_back.at[k], r_back.at[slot], level(k))
-
-    def back_plane(p, slot):
-        return remote(whole, result.at[core * PLANE + slot], s_wide.at[p], r_wide.at[slot], chip(p))
-
-    def back_mate(p, half):
-        at = half * PLANE + p
-        return remote(result.at[at], result.at[at], s_last.at[p], r_last.at[p], mate)
-
-    def each(count, mine, body, first=1, last=None):
-        def step(k, _):
-            body(lax.rem(mine + k, count))
-            return 0
-
-        lax.fori_loop(first, count if last is None else last, step, 0)
-
-    each(PLANE, me, lambda p: to_mate(p).start(), 1, PLANE + 1)
-
-    def pair_sum(p):
-        to_mate(p).wait_recv()
-        paired[p] = packed[core * PLANE + p] + mate_in[p]
-
-    def pair_and_send(p):
-        pair_sum(p)
-        to_plane(p, me).start()
-
-    each(PLANE, me, pair_and_send)
-    pair_sum(me)
-
-    def gather_plane(k, total):
-        p = lax.rem(me + k, PLANE)
-        to_plane(p, p).wait_recv()
-        return total + plane_in[p]
-
-    total = lax.fori_loop(1, PLANE, gather_plane, paired[me])
-    for k in range(DEEP):
-        deep_out[k] = total[3 * k:3 * k + 3, :]
-    each(DEEP, z, lambda k: to_level(k, z).start())
-
-    def gather_level(step, total):
-        k = lax.rem(z + step, DEEP)
-        to_level(k, k).wait_recv()
-        return total + deep_in[k]
-
-    part[...] = lax.fori_loop(1, DEEP, gather_level, deep_out[z])
-
-    each(DEEP, z, lambda k: back_level(k, z).start())
-    deep_back[z] = part[...]
-    each(DEEP, z, lambda k: back_level(k, k).wait_recv())
-    for k in range(DEEP):
-        whole[3 * k:3 * k + 3, :] = deep_back[k]
-    each(PLANE, me, lambda p: back_plane(p, me).start())
-    result[core * PLANE + me] = whole[...]
-    back_mate(me, core).start()
-
-    def forward(p):
-        back_plane(p, p).wait_recv()
-        back_mate(p, core).start()
-
-    each(PLANE, me, forward)
-    each(PLANE, me, lambda p: back_mate(p, 1 - core).wait_recv(), 0)
-
-    each(PLANE, me, lambda p: to_mate(p).wait_send(), 0)
-    each(PLANE, me, lambda p: to_plane(p, me).wait_send())
-    each(DEEP, z, lambda k: to_level(k, z).wait_send())
-    each(DEEP, z, lambda k: back_level(k, z).wait_send())
-    each(PLANE, me, lambda p: back_plane(p, me).wait_send())
-    each(PLANE, me, lambda p: back_mate(p, core).wait_send(), 0)
+    lax.fori_loop(0, 24, greet, 0)
+
+    arguments = [(source, lines.at[k]) for k, source in enumerate((owner, local, anchor, frac_x, frac_y, label))]
+    arguments += [(raster, raster_in), (beta, beta_in)]
+    copies = [pltpu.make_async_copy(source, target, loads.at[k]) for k, (source, target) in enumerate(arguments)]
+    for copy in copies:
+        copy.start()
+    for copy in copies[:6]:
+        copy.wait()
+    message, slot = request_rows(*[lines[k] for k in range(6)])
+    slot_out[...] = slot
+    for k in range(OWNERS):
+        out_codes[k] = message[k:k + 1, :]
+    copies[6].wait()
+    copies[7].wait()
+    swap_rows_and_tiles(raster_in, turned)
+    pl.semaphore_wait(barrier, OWNERS - 1 + 24 + 1)
+    exchange(tile, rep, out_codes, came, send_sem, recv_sem)
+    arrived = jnp.concatenate([came[k] for k in range(OWNERS)], axis=0)
+    codes[...] = jnp.concatenate([arrived, pltpu.roll(arrived, 128 - 12, 1)], axis=0).T
+    form_terms(codes, beta_in, packed, rows_out, turned, scaled, resid)
+    add_up((me, core, pair, mate, chip, level), packed, mate_in, paired, group_in, mine, level_in, whole, result, sems)
 
     def write(k, _):
         out[k] = result[k]
         return 0
 
-    lax.fori_loop(0, 32, write, 0)
-
-
-def total(packed):
-    dma = pltpu.SemaphoreType.DMA((PLANE,))
-    f32 = jnp.float32
+    lax.fori_loop(0, 2 * GROUP, write, 0)
+
+
+def sums(lines, raster, beta):
+    f32, bf16, i32 = jnp.float32, jnp.bfloat16, jnp.int32
+    group = pltpu.SemaphoreType.DMA((GROUP,))
+    deep = pltpu.SemaphoreType.DMA((LEVELS,))
+    tiles = pltpu.SemaphoreType.DMA((OWNERS,))
     return pl.pallas_call(
-        total_kernel,
-        out_shape=jax.ShapeDtypeStruct((32, ROWS, 128), f32),
-        in_specs=[VMEM],
-        out_specs=VMEM,
+        sums_kernel,
+        out_shape=(
+            jax.ShapeDtypeStruct((2 * GROUP, ROWS, 128), f32),
+            jax.ShapeDtypeStruct((BASIS, OWNERS * SLOTS), bf16),
+            jax.ShapeDtypeStruct((1, FIXES), f32),
+        ),
+        in_specs=[pl.BlockSpec(memory_space=pltpu.HBM)] * 8,
+        out_specs=(VMEM, VMEM, VMEM),
         scratch_shapes=[
-            pltpu.VMEM((PLANE, ROWS, 128), f32),
-            pltpu.VMEM((PLANE, ROWS, 128), f32),
-            pltpu.VMEM((PLANE, ROWS, 128), f32),
-            pltpu.VMEM((DEEP, 3, 128), f32),
-            pltpu.VMEM((DEEP, 3, 128), f32),
-            pltpu.VMEM((3, 128), f32),
-            pltpu.VMEM((DEEP, 3, 128), f32),
+            pltpu.VMEM((6, 1, FIXES), i32),
+            pltpu.VMEM((16, LAYERS, 256), bf16),
+            pltpu.VMEM((1, BASIS), f32),
+            pltpu.VMEM((OWNERS, 1, 128), f32),
+            pltpu.VMEM((OWNERS, 1, 128), f32),
+            pltpu.VMEM((128, 128), f32),
+            pltpu.VMEM((1024, 256), bf16),
+            pltpu.VMEM((BASIS, OWNERS * SLOTS), bf16),
+            pltpu.VMEM((16, OWNERS * SLOTS), bf16),
+            pltpu.VMEM((2 * GROUP, ROWS, 128), f32),
+            pltpu.VMEM((GROUP, ROWS, 128), f32),
+            pltpu.VMEM((GROUP, ROWS, 128), f32),
+            pltpu.VMEM((GROUP, ROWS, 128), f32),
             pltpu.VMEM((ROWS, 128), f32),
-            pltpu.VMEM((32, ROWS, 128), f32),
-        ] + [dma] * 12,
-        compiler_params=pltpu.CompilerParams(collective_id=1, has_side_effects=True, vmem_limit_bytes=LIMIT),
-    )(packed)
+            pltpu.VMEM((LEVELS, ROWS, 128), f32),
+            pltpu.VMEM((ROWS, 128), f32),
+            pltpu.VMEM((2 * GROUP, ROWS, 128), f32),
+            pltpu.SemaphoreType.DMA((8,)),
+            tiles, tiles, group, group, group, group, deep, deep, group, group, group, group,
+        ],
+        compiler_params=pltpu.CompilerParams(collective_id=0, has_side_effects=True, vmem_limit_bytes=LIMIT),
+    )(*lines, raster, beta)
 
 
 def reciprocal(x):
@@ -406,21 +397,21 @@
     return inner
 
 
-def solve_kernel(sums, smooth, beta_new, system, scaled, right):
+def solve_system(sums, smooth, beta_new, system, scaled, right):
     count = 1.0 / (FIXES * 512.0)
     lane, row = iota((8, 128), 1), iota((8, 128), 0)
     inner = second_difference()
     tile = 0
     for i, j in BLOCKS:
         for r in range(16):
-            value = sums[tile // 5, tile % 5 * 8:tile % 5 * 8 + 8, :] * count
+            value = sums[tile // 3, tile % 3 * 8:tile % 3 * 8 + 8, :] * count
             if i == j:
                 value = value + jnp.where(lane // 8 == r, smooth[16 * i + r] * inner, 0.0)
                 value = value + jnp.where(lane == row + 8 * r, RIDGE, 0.0)
             system[i, r * 8:r * 8 + 8, j * 128:(j + 1) * 128] = value
             tile += 1
     for part in range(4):
-        right[part] = sums[part, 40:41, :] * count
+        right[part] = sums[GRAM_TILES // 3, TARGET_ROW + part:TARGET_ROW + part + 1, :] * count
 
     inverse = []
     done = []
@@ -447,21 +438,6 @@
         beta_new[:, k * 128:(k + 1) * 128] = found[k][0:1, :]
 
 
-def solve(sums, smooth):
-    return pl.pallas_call(
-        solve_kernel,
-        out_shape=jax.ShapeDtypeStruct((1, BASIS), jnp.float32),
-        in_specs=[VMEM, SMEM],
-        out_specs=VMEM,
-        scratch_shapes=[
-            pltpu.VMEM((4, 128, BASIS), jnp.float32),
-            pltpu.VMEM((4, 128, BASIS), jnp.float32),
-            pltpu.VMEM((4, 1, 128), jnp.float32),
-        ],
-        compiler_params=pltpu.CompilerParams(vmem_limit_bytes=LIMIT),
-    )(sums, smooth)
-
-
 def predict_rows(rows, beta_new):
     eta = jnp.sum(dot(stacked_thirds(beta_new), rows), axis=0, keepdims=True)
     lines = [eta[:, b * 128:(b + 1) * 128] for b in range(12)]
@@ -478,10 +454,11 @@
     return jnp.sum(jnp.where(at, spread[:SLOTS], 0.0), axis=0, keepdims=True)
 
 
-def predict_kernel(rows, beta_new, owner, slot, eta_new, out, came, send_sem, recv_sem):
+def finish_kernel(sums, smooth, rows, owner, slot, beta_new, eta_new, system, scaled, right, out, came, send_sem, recv_sem):
     tile, rep = position()
     barrier = pltpu.get_barrier_semaphore()
     greet_tile(barrier, tile, rep)
+    solve_system(sums, smooth, beta_new, system, scaled, right)
     message = predict_rows(rows[...], beta_new[...])
     for k in range(OWNERS):
         out[k] = message[k:k + 1, :]
@@ -491,29 +468,30 @@
     eta_new[...] = unpack_rows(arrived, owner[...], slot[...])
 
 
-def predict(rows, beta_new, owner, slot):
+def finish(sums, smooth, rows, owner, slot):
+    f32 = jnp.float32
+    tiles = pltpu.SemaphoreType.DMA((OWNERS,))
     return pl.pallas_call(
-        predict_kernel,
-        out_shape=jax.ShapeDtypeStruct((1, FIXES), jnp.float32),
-        in_specs=[VMEM] * 4,
-        out_specs=VMEM,
+        finish_kernel,
+        out_shape=(jax.ShapeDtypeStruct((1, BASIS), f32), jax.ShapeDtypeStruct((1, FIXES), f32)),
+        in_specs=[VMEM, SMEM, VMEM, VMEM, VMEM],
+        out_specs=(VMEM, VMEM),
         scratch_shapes=[
-            pltpu.VMEM((OWNERS, 1, 128), jnp.float32),
-            pltpu.VMEM((OWNERS, 1, 128), jnp.float32),
-            pltpu.SemaphoreType.DMA((OWNERS,)),
-            pltpu.SemaphoreType.DMA((OWNERS,)),
+            pltpu.VMEM((4, 128, BASIS), f32),
+            pltpu.VMEM((4, 128, BASIS), f32),
+            pltpu.VMEM((4, 1, 128), f32),
+            pltpu.VMEM((OWNERS, 1, 128), f32),
+            pltpu.VMEM((OWNERS, 1, 128), f32),
+            tiles, tiles,
         ],
-        compiler_params=pltpu.CompilerParams(collective_id=2, has_side_effects=True, vmem_limit_bytes=LIMIT),
-    )(rows, beta_new, owner, slot)
+        compiler_params=pltpu.CompilerParams(collective_id=1, has_side_effects=True, vmem_limit_bytes=LIMIT),
+    )(sums, smooth, rows, owner, slot)
 
 
 def shards(owner, tile_local, anchor, frac_x, frac_y, label, raster, beta, smooth):
-    line = lambda array: array.reshape(1, FIXES)
-    owner = line(owner)
-    codes, slot = request([owner] + [line(a) for a in (tile_local, anchor, frac_x, frac_y, label)])
-    packed, rows = terms(codes, raster, beta.reshape(1, BASIS))
-    beta_new = solve(total(packed), smooth)
-    eta_new = predict(rows, beta_new, owner, slot)
+    lines = [array.reshape(1, FIXES) for array in (owner, tile_local, anchor, frac_x, frac_y, label)]
+    added, rows, slot = sums(lines, raster, beta.reshape(1, BASIS))
+    beta_new, eta_new = finish(added, smooth, rows, lines[0], slot)
     return beta_new.reshape(BASIS), eta_new.reshape(FIXES)
 
 

time: 130 us -> 111 us (0.85)
  Pallas kernels: 122 us -> 108 us
  local copies, waits for them, and re-layouts: 7.07 us -> 2.49 us
    pallas_call x5 -> x2, Pallas kernels: 122 us -> 108 us  [the longest x1 67.9 us: sums(): pl.pallas_call(sums_kernel, out_shape=(jax.ShapeDtypeStruct((2 * GROUP, R...]
    unnamed x21 -> x2, local copies, waits for them, and re-layouts: 7.07 us -> 2.49 us
where the time goes in v2:
time: 111 us
  Pallas kernels  108 us (97%)
  local copies, waits for them, and re-layouts  2.49 us (2%)
    pallas_call x1, Pallas kernels, sums(): pl.pallas_call(sums_kernel, out_shape=(jax.ShapeDtypeStruct((2 * GROUP, R...  67.9 us
    pallas_call x1, Pallas kernels, finish(): pl.pallas_call(finish_kernel, out_shape=(jax.ShapeDtypeStruct((1, BASIS),...  39.9 us
    unnamed x2, local copies, waits for them, and re-layouts  2.49 us

profile of v2, /device:TPU:1, one launch (start us, length us, event | category | flops | bytes accessed | tf_op | source)
XLA Modules:
  0.0 110.9 jit_solution(2012306712856858361)
XLA Ops:
  0.6 67.9 %shard_map.104 = (f32[64,24,128]{2,1,0:T(8,128)}, bf16[512,1536]{1,0:T(8,128)(2,1)}, f32[1,512]{1,0:T(1,128)}) custom-call(s32[1,512]{1,0:T(1,128)} %bitcast.9, s32[1,512]{1,0:T(1,128)} %bitcast.11, s32[1,512]{1,0:T(1,128)} %bitcast.12, s32[1,512]{1,0:T(1,128)} %bitcast.13, s32[1,512]{1,0:T(1,128)} %bitcast.14, s32[1,512]{1,0:T(1,128)} %bitcast.15, ...), custom_call_target="tpu_custom_call" | custom-call | tf_op jit(solution)/shard_map/pallas_call | solution.py:310
  68.5 39.9 %shard_map.105 = (f32[1,512]{1,0:T(1,128)}, f32[1,512]{1,0:T(1,128)}) custom-call(f32[64,24,128]{2,1,0:T(8,128)} %get-tuple-element.7.sums, f32[64]{0:T(128)} %smooth.1, bf16[512,1536]{1,0:T(8,128)(2,1)} %get-tuple-element.8.rows, s32[1,512]{1,0:T(1,128)} %bitcast.10, f32[1,512]{1,0:T(1,128)} %get-tuple-element.9.slot), custom_call_target="tpu_custom_call" | custom-call | tf_op jit(solution)/shard_map/pallas_call | solution.py:474
  108.4 1.2 %copy.13 = f32[512]{0:T(512)} copy(f32[512]{0:T(512)} %bitcast.18) | data formatting | bytes 4096
  109.7 1.3 %copy.14 = f32[512]{0:T(512)} copy(f32[512]{0:T(512)} %bitcast.17) | data formatting | bytes 4096

commit v3 on v2

v3 whole, which is shorter than its diff:
```python
import functools

import jax
import jax.numpy as jnp
from jax import lax
from jax.experimental import pallas as pl
from jax.experimental.pallas import tpu as pltpu
from jax.sharding import PartitionSpec as P

SPLINES = 8
RIDGE = 0.002
LAYERS = 64
BASIS = 512
FIXES = 512
SLOTS = 24
OWNERS = 64
DEEP = 16
GROUP = 32
LEVELS = 8
ROWS = 24
GRAM_TILES = 160
TARGET_ROW = GRAM_TILES % 3 * 8
REACH = 2.5
STEPS = 13104.0
MESH = pl.DeviceIdType.MESH
HIGHEST = lax.Precision.HIGHEST
VMEM = pl.BlockSpec(memory_space=pltpu.VMEM)
SMEM = pl.BlockSpec(memory_space=pltpu.SMEM)
LIMIT = 62 * 1024 * 1024
BLOCKS = [(i, j) for i in range(4) for j in range(i, 4)]
NT = (((1,), (1,)), ((), ()))
TN = (((0,), (0,)), ((), ()))


def dot(a, b, dims=(((1,), (0,)), ((), ())), precision=None):
    return lax.dot_general(a, b, dims, precision=precision, preferred_element_type=jnp.float32)


def iota(shape, axis):
    return lax.broadcasted_iota(jnp.int32, shape, axis)


def thirds(x):
    high = x.astype(jnp.bfloat16)
    rest = x - high.astype(jnp.float32)
    mid = rest.astype(jnp.bfloat16)
    low = (rest - mid.astype(jnp.float32)).astype(jnp.bfloat16)
    return high, mid, low


def stacked_thirds(x):
    high, mid, low = thirds(x)
    row = iota((16, x.shape[1]), 0)
    wide = lambda part: jnp.broadcast_to(part.astype(jnp.float32), row.shape)
    parts = jnp.where(row == 0, wide(high), jnp.where(row == 1, wide(mid), jnp.where(row == 2, wide(low), 0.0)))
    return parts.astype(jnp.bfloat16)


def remote(src, dst, send, recv, device):
    return pltpu.make_async_remote_copy(
        src_ref=src, dst_ref=dst, send_sem=send, recv_sem=recv, device_id=device, device_id_type=MESH)


def position():
    return lax.axis_index("tile"), lax.axis_index("rep")


def request_rows(owner, local, anchor, frac_x, frac_y, label):
    named = (iota((OWNERS, FIXES), 0) == owner).astype(jnp.float32)
    named_b = named.astype(jnp.bfloat16)
    earlier = (iota((FIXES, FIXES), 0) < iota((FIXES, FIXES), 1)).astype(jnp.float32).astype(jnp.bfloat16)
    before = dot(named_b, earlier)
    slot = jnp.sum(before * named, axis=0, keepdims=True)
    at = iota((SLOTS, FIXES), 0).astype(jnp.float32) == slot
    fields = [field.astype(jnp.float32) for field in (local, anchor, frac_x, frac_y, label + 1)]
    spread = [jnp.where(at, field, 0.0) for field in fields] + [jnp.zeros((8, FIXES), jnp.float32)]
    spread = jnp.concatenate(spread, axis=0).astype(jnp.bfloat16)
    return dot(named_b, spread, NT), slot


def greet_tile(barrier, tile, rep):
    def greet(step, _):
        pl.semaphore_signal(barrier, inc=1, device_id=(lax.rem(tile + step, OWNERS), rep), device_id_type=MESH)
        return 0

    lax.fori_loop(1, OWNERS, greet, 0)


def send_all(tile, rep, out, came, send_sem, recv_sem):
    def begin(step, _):
        peer = lax.rem(tile + step, OWNERS)
        remote(out.at[peer], came.at[tile], send_sem, recv_sem, (peer, rep)).start()
        return 0

    lax.fori_loop(1, OWNERS, begin, 0)
    came[tile] = out[tile]


def all_messages(tile, rep, out, came, send_sem, recv_sem):
    many = pl.ds(0, OWNERS - 1)
    return remote(out.at[many], came.at[many], send_sem, recv_sem, (lax.rem(tile + 1, OWNERS), rep))


def swap_rows_and_tiles(raster, turned):
    group = iota((LAYERS, 128), 1) // 16
    for half in range(2):
        for part in range(2):
            held = [raster[8 * part + t, :, half * 128:(half + 1) * 128].astype(jnp.float32) for t in range(8)]
            for step in (1, 2, 4):
                upper = (group // step) % 2 == 1
                for t in range(8):
                    if t & step == 0:
                        a, b = held[t], held[t | step]
                        held[t] = jnp.where(upper, pltpu.roll(b, 16 * step, 1), a)
                        held[t | step] = jnp.where(upper, b, pltpu.roll(a, 128 - 16 * step, 1))
            for r in range(8):
                row = 8 * half + r
                turned[row * 64:(row + 1) * 64, part * 128:(part + 1) * 128] = held[r].astype(jnp.bfloat16)


def expand(values):
    shape = (LAYERS, SPLINES, values.shape[1])
    spread = jnp.broadcast_to(values[:, None, :], shape)
    knots = 0.5 * (iota(shape, 1).astype(jnp.float32) - 0.5 * (SPLINES - 1))
    bump = jnp.maximum(1.0 - jnp.abs(spread - knots) * (1.0 / 0.75), 0.0)
    return (bump * bump * bump).reshape(BASIS, values.shape[1]).astype(jnp.bfloat16)


def form_terms(codes, beta, packed, coded, rows_out, turned, scaled, resid):
    beta_parts = stacked_thirds(beta[...])

    def block(at):
        def field(f):
            return jnp.concatenate([codes[pl.ds(f * SLOTS + 2 * at, 1), :], codes[pl.ds(f * SLOTS + 2 * at + 1, 1), :]], axis=1)

        local, anchor, frac_x, frac_y, mark = [field(f) for f in range(5)]
        row = jnp.floor((anchor + 0.5) * (1.0 / 15.0))
        cell = local * 16.0 + (anchor - 15.0 * row)
        lane = iota((256, 256), 0).astype(jnp.float32)
        weight_x = jnp.where(lane == cell, 256.0 - frac_x, 0.0) + jnp.where(lane == cell + 1.0, frac_x, 0.0)
        along = dot(turned[...], weight_x.astype(jnp.bfloat16))
        values = None
        for r in range(16):
            weight_y = jnp.where(row == float(r), 256.0 - frac_y, 0.0) + jnp.where(row == float(r - 1), frac_y, 0.0)
            term = weight_y * along[r * 64:(r + 1) * 64]
            values = term if values is None else values + term
        values = values * (1.0 / 65536.0)
        lanes = pl.ds(pl.multiple_of(at * 256, 256), 256)
        coded[:, lanes] = jnp.floor(jnp.clip(values, -REACH, REACH) * STEPS + 0.5).astype(jnp.int32)
        rows = expand(values)
        rows_out[:, lanes] = rows
        eta = jnp.sum(dot(beta_parts, rows), axis=0, keepdims=True)
        live = (mark > 0.5).astype(jnp.float32)
        outcome = mark - 1.0
        prob = 1.0 / (1.0 + jnp.exp(-eta))
        weight = prob * (1.0 - prob) * live
        scaled[:, lanes] = (jnp.sqrt(weight) * rows.astype(jnp.float32)).astype(jnp.bfloat16)
        resid[:, lanes] = stacked_thirds(weight * eta + (outcome - prob) * live)

    pl.loop(0, 6)(block)
    target = jnp.sum(dot(resid[...], rows_out[...], NT), axis=0, keepdims=True)
    for spare in range(GRAM_TILES, 2 * GROUP * 3):
        packed[spare // 3, spare % 3 * 8:spare % 3 * 8 + 8, :] = jnp.zeros((8, 128), jnp.float32)
    for part in range(4):
        packed[GRAM_TILES // 3, TARGET_ROW + part:TARGET_ROW + part + 1, :] = target[:, part * 128:(part + 1) * 128]
    tile = 0
    for i in range(4):
        panel = dot(scaled[i * 128:(i + 1) * 128, :], scaled[i * 128:, :], NT)
        for j in range(i, 4):
            for r in range(16):
                packed[tile // 3, tile % 3 * 8:tile % 3 * 8 + 8, :] = panel[r * 8:r * 8 + 8, (j - i) * 128:(j - i + 1) * 128]
                tile += 1


def add_up(place, packed, mate_in, paired, group_in, mine, level_in, whole, result, sems, while_down, while_back):
    s_mate, r_mate, s_group, r_group, s_level, r_level, s_wide, r_wide, s_last, r_last = sems
    me, core, pair, mate, chip, level = place
    peer = chip(lax.rem(me + 1, GROUP))
    most = pl.ds(0, GROUP - 1)

    def to_mate(p):
        return remote(packed.at[(1 - core) * GROUP + p], mate_in.at[p], s_mate, r_mate.at[p], mate)

    def back_chip(p, slot):
        return remote(whole, result.at[core * GROUP + slot], s_wide.at[p], r_wide.at[slot], chip(p))

    def back_mate(p):
        at = core * GROUP + p
        return remote(result.at[at], result.at[at], s_last, r_last, mate)

    def each(body, first=1, last=GROUP):
        def step(k, _):
            body(lax.rem(me + k, GROUP))
            return 0

        lax.fori_loop(first, last, step, 0)

    each(lambda p: to_mate(p).start(), 1, GROUP + 1)

    def pair_sum(p):
        to_mate(p).wait_recv()
        paired[p] = packed[core * GROUP + p] + mate_in[p]

    def pair_and_send(p):
        pair_sum(p)
        remote(paired.at[p], group_in.at[me], s_group, r_group, chip(p)).start()

    each(pair_and_send)
    pair_sum(me)
    group_in[me] = paired[me]
    while_down()
    all_group = remote(paired.at[most], group_in.at[most], s_group, r_group, peer)
    all_group.wait_recv()

    def gather(k, total):
        return total + (group_in[4 * k] + group_in[4 * k + 1]) + (group_in[4 * k + 2] + group_in[4 * k + 3])

    mine[...] = lax.fori_loop(0, GROUP // 4, gather, jnp.zeros((ROWS, 128), jnp.float32))
    others = [lax.rem(pair + step, LEVELS) for step in (4, 3, 5, 2, 6, 1, 7)]
    for k in others:
        remote(mine, level_in.at[pair], s_level.at[k], r_level.at[pair], level(k)).start()
    level_in[pair] = mine[...]
    for k in others:
        remote(mine, level_in.at[k], s_level.at[k], r_level.at[k], level(k)).wait_recv()
    total = level_in[0]
    for k in range(1, LEVELS):
        total = total + level_in[k]
    whole[...] = total

    each(lambda p: back_chip(p, me).start())
    result[core * GROUP + me] = total
    back_mate(me).start()
    while_back()

    def forward(p):
        back_chip(p, p).wait_recv()
        back_mate(p).start()

    each(forward)
    theirs = result.at[pl.ds((1 - core) * GROUP, GROUP)]
    remote(theirs, theirs, s_last, r_last, mate).wait_recv()

    def settle():
        remote(mate_in, mate_in, s_mate, s_mate, mate).wait_send()
        all_group.wait_send()
        for k in others:
            remote(mine, level_in.at[k], s_level.at[k], r_level.at[k], level(k)).wait_send()
        each(lambda p: back_chip(p, me).wait_send())
        remote(theirs, theirs, s_last, r_last, mate).wait_send()

    return settle


def pack_values(coded, out):
    for t in range(3):
        words = []
        for r in (2 * t, 2 * t + 1):
            low, high = coded[:, r * 128:(r + 1) * 128], coded[:, (r + 6) * 128:(r + 7) * 128]
            words.append((low & 65535) | (high << 16))
        turned = jnp.concatenate(words, axis=0).T
        for k in range(OWNERS):
            out[k, 2 * t:2 * t + 1, :] = turned[k:k + 1, :]
            out[k, 2 * t + 1:2 * t + 2, :] = turned[OWNERS + k:OWNERS + k + 1, :]


def unpack_words(came, bytes_out, t):
    words = jnp.concatenate([came[k, 2 * t + half:2 * t + half + 1, :] for half in range(2) for k in range(OWNERS)], axis=0).T
    for which, codes in enumerate(((words << 16) >> 16, words >> 16)):
        for r in range(2):
            code = codes[r * 64:(r + 1) * 64, :]
            upper, lower = code >> 8, code & 255
            both = jnp.concatenate([upper, lower], axis=0).astype(jnp.float32).astype(jnp.bfloat16)
            block = 6 * which + 2 * t + r
            bytes_out[:, block * 128:(block + 1) * 128] = both


def values_of_fixes(bytes_in, owner, slot):
    second = slot >= 12.0
    key = jnp.where(second, (slot - 12.0) * 128.0 + 64.0, slot * 128.0) + owner.astype(jnp.float32)
    place = iota((OWNERS * SLOTS, key.shape[1]), 0).astype(jnp.float32)
    picked = dot(bytes_in[...], (place == key).astype(jnp.float32).astype(jnp.bfloat16))
    return (picked[:LAYERS] * 256.0 + picked[LAYERS:]) * (1.0 / STEPS)


def reciprocal(x):
    guess = pltpu.reciprocal(x, approx=True)
    return guess * (2.0 - x * guess)


def add_tree(terms):
    while len(terms) > 1:
        terms = [terms[k] + terms[k + 1] if k + 1 < len(terms) else terms[k] for k in range(0, len(terms), 2)]
    return terms[0]


def six_left(x):
    high, mid, low = thirds(x)
    return jnp.concatenate([high, high, high, mid, mid, low], axis=1)


def six_right(x):
    high, mid, low = thirds(x)
    return jnp.concatenate([high, mid, low, high, mid, high], axis=0)


def invert(tiles, chores):
    tiles, chores = list(tiles), list(chores)
    share = -(-len(chores) // 15)
    lane = iota((8, 128), 1)
    row = iota((8, 128), 0)

    def take(tile, m):
        return jnp.broadcast_to(tile[m:m + 1, :], (8, 128))

    def column(tile, at):
        return jnp.broadcast_to(tile[:, at:at + 1], (8, 128))

    for b in range(16):
        inside = (lane // 8) == b
        columns = [column(tiles[b], 8 * b + m) for m in range(8)]
        lead = jnp.where(inside, jnp.where(lane - 8 * b == row, 1.0, 0.0), tiles[b])
        for m in range(0, 8, 2):
            p, q, r = take(columns[m], m), take(columns[m + 1], m), take(columns[m + 1], m + 1)
            scale = reciprocal(p * r - q * q)
            is_first, is_second = row == m, row == m + 1

            def sweep(tile):
                first, second = take(tile, m), take(tile, m + 1)
                first, second = r * first - q * second, p * second - q * first
                rest = tile - (columns[m] * first + columns[m + 1] * second) * scale
                return jnp.where(is_first, first * scale, jnp.where(is_second, second * scale, rest))

            later = [sweep(columns[k]) for k in range(m + 2, 8)]
            lead = sweep(lead)
            columns = columns[:m + 2] + later
        taken = [take(lead, m) for m in range(8)]
        order = [(b + 1 + s) % 16 for s in range(15)]
        far = order[8:]
        left = jnp.concatenate([jnp.where(inside, tiles[i], 0.0) for i in far], axis=0)
        blank = lambda n: [jnp.zeros((8 * n, 128), jnp.float32)] if n else []
        change = dot(six_left(left), six_right(jnp.concatenate(blank(b) + [lead] + blank(15 - b), axis=0)))
        for i in order[:8]:
            terms = [column(tiles[i], 8 * b + m) * taken[m] for m in range(8)]
            tiles[i] = jnp.where(inside, 0.0, tiles[i]) - add_tree(terms)
        for s, i in enumerate(far):
            tiles[i] = jnp.where(inside, 0.0, tiles[i]) - change[8 * s:8 * s + 8, :]
        tiles[b] = lead
        for chore in chores[b * share:(b + 1) * share]:
            chore()
    return tiles


def second_difference():
    i, j = iota((8, 128), 0), iota((8, 128), 1) % 8
    inner = jnp.zeros((8, 128), jnp.float32)

    def entry(at, r):
        return jnp.where(at == r, 1.0, 0.0) - jnp.where(at == r + 1, 2.0, 0.0) + jnp.where(at == r + 2, 1.0, 0.0)

    for r in range(SPLINES - 2):
        inner = inner + entry(i, r) * entry(j, r)
    return inner


def solve_system(sums, smooth, beta_new, system, spread, late_chores):
    count = 1.0 / (FIXES * 512.0)
    lane, row = iota((8, 128), 1), iota((8, 128), 0)
    inner = second_difference()
    tile = 0
    for i, j in BLOCKS:
        for r in range(16):
            value = sums[tile // 3, tile % 3 * 8:tile % 3 * 8 + 8, :] * count
            if i == j:
                value = value + jnp.where(lane // 8 == r, smooth[16 * i + r] * inner, 0.0)
                value = value + jnp.where(lane == row + 8 * r, RIDGE, 0.0)
            system[i, r * 8:r * 8 + 8, j * 128:(j + 1) * 128] = value
            tile += 1
    for part in range(4):
        line = sums[GRAM_TILES // 3, TARGET_ROW + part:TARGET_ROW + part + 1, :] * count
        system[part, :, 512:640] = jnp.broadcast_to(line, (128, 128)).T

    def spread_of(k, inverse, start, stop):
        part = dot(inverse, six_right(system[k, :, start:stop]))
        system[k, :, start:stop] = part
        spread[:, start:stop] = six_right(part)

    def eliminate(i, left, start, stop):
        system[i, :, start:stop] = system[i, :, start:stop] - dot(left, spread[:, start:stop])

    pending = []
    for k in range(4):
        diagonal = [system[k, r * 8:r * 8 + 8, k * 128:(k + 1) * 128] for r in range(16)]
        inverse = six_left(jnp.concatenate(invert(diagonal, pending), axis=0))
        near = (k + 1) * 128
        lefts = {i: six_left(system[k, :, i * 128:(i + 1) * 128].T) for i in range(k + 1, 4)}
        lefts.update({i: six_left(system[i, :, k * 128:(k + 1) * 128]) for i in range(k)})
        spread_of(k, inverse, near, near + 128)
        pending = []
        if k < 3:
            eliminate(k + 1, lefts[k + 1], near, near + 128)
            pending.append(functools.partial(spread_of, k, inverse, near + 128, 640))
            pending.append(functools.partial(eliminate, k + 1, lefts[k + 1], near + 128, 640))
            for i in range(k + 2, 4):
                pending.append(functools.partial(eliminate, i, lefts[i], i * 128, 640))
            for i in range(k):
                pending.append(functools.partial(eliminate, i, lefts[i], near, 640))
        else:
            for i in range(k):
                eliminate(i, lefts[i], 512, 640)
        if k == 2:
            pending += late_chores
    for k in range(4):
        beta_new[:, k * 128:(k + 1) * 128] = system[k, :, 512:640].T[0:1, :]


def step_kernel(owner, local, anchor, frac_x, frac_y, label, raster, beta, smooth, beta_new, eta_new,
                lines, raster_in, beta_in, out_codes, came, codes, turned, rows, scaled, resid, coded,
                packed, mate_in, paired, group_in, mine, level_in, whole, result,
                out_values, came_values, value_bytes, own_rows, slot_row, system, spread,
                loads, send_codes, recv_codes, send_values, recv_values, *sems):
    tile, rep = position()
    x, z = lax.div(tile, DEEP), lax.rem(tile, DEEP)
    y, core = lax.div(rep, 2), lax.rem(rep, 2)
    pair, low = lax.div(z, 2), lax.rem(z, 2)
    me = (x * 4 + y) * 2 + low
    mate = (tile, rep + 1 - 2 * core)

    def chip(p):
        return (lax.div(p, 8) * DEEP + pair * 2 + lax.rem(p, 2), lax.rem(lax.div(p, 2), 4) * 2 + core)

    def level(k):
        return (x * DEEP + k * 2 + low, rep)

    barrier = pltpu.get_barrier_semaphore()
    greet_tile(barrier, tile, rep)
    pl.semaphore_signal(barrier, inc=1, device_id=mate, device_id_type=MESH)

    def greet(step, _):
        other_y = lax.rem(y + 1 + lax.rem(step, 3), 4)
        rest = lax.div(step, 3)
        device = (lax.div(rest, 2) * DEEP + pair * 2 + lax.rem(rest, 2), other_y * 2 + core)
        pl.semaphore_signal(barrier, inc=1, device_id=device, device_id_type=MESH)
        return 0

    lax.fori_loop(0, 24, greet, 0)

    arguments = [(source, lines.at[k]) for k, source in enumerate((owner, local, anchor, frac_x, frac_y, label))]
    arguments += [(raster, raster_in), (beta, beta_in)]
    copies = [pltpu.make_async_copy(source, target, loads.at[k]) for k, (source, target) in enumerate(arguments)]
    for copy in copies:
        copy.start()
    for copy in copies[:6]:
        copy.wait()
    message, slot = request_rows(*[lines[k] for k in range(6)])
    slot_row[...] = slot
    for k in range(OWNERS):
        out_codes[k] = message[k:k + 1, :]
    copies[6].wait()
    copies[7].wait()
    swap_rows_and_tiles(raster_in, turned)
    pl.semaphore_wait(barrier, OWNERS - 1 + 24 + 1)

    codes_sent = (tile, rep, out_codes, came, send_codes, recv_codes)
    send_all(*codes_sent)
    all_messages(*codes_sent).wait_recv()
    arrived = jnp.concatenate([came[k] for k in range(OWNERS)], axis=0)
    codes[...] = jnp.concatenate([arrived, pltpu.roll(arrived, 128 - 12, 1)], axis=0).T
    form_terms(codes, beta_in, packed, coded, rows, turned, scaled, resid)

    values_sent = (tile, rep, out_values, came_values, send_values, recv_values)
    settle = add_up(
        (me, core, pair, mate, chip, level), packed, mate_in, paired, group_in, mine, level_in, whole, result, sems,
        lambda: pack_values(coded, out_values), lambda: send_all(*values_sent))

    def place_rows(part):
        values = values_of_fixes(value_bytes, lines[0, :, part * 128:(part + 1) * 128], slot_row[:, part * 128:(part + 1) * 128])
        own_rows[:, part * 128:(part + 1) * 128] = expand(values)

    chores = [settle, lambda: all_messages(*codes_sent).wait_send(), lambda: all_messages(*values_sent).wait_recv()]
    chores += [functools.partial(unpack_words, came_values, value_bytes, t) for t in range(3)]
    chores += [functools.partial(place_rows, part) for part in range(4)]
    solve_system(result, smooth, beta_new, system, spread, chores)
    eta_new[...] = jnp.sum(dot(stacked_thirds(beta_new[...]), own_rows[...]), axis=0, keepdims=True)
    all_messages(*values_sent).wait_send()


def step(lines, raster, beta, smooth):
    f32, bf16, i32 = jnp.float32, jnp.bfloat16, jnp.int32
    one = pltpu.SemaphoreType.DMA
    group = pltpu.SemaphoreType.DMA((GROUP,))
    deep = pltpu.SemaphoreType.DMA((LEVELS,))
    chunks = pltpu.VMEM((GROUP, ROWS, 128), f32)
    chunk = pltpu.VMEM((ROWS, 128), f32)
    served = OWNERS * SLOTS
    return pl.pallas_call(
        step_kernel,
        out_shape=(jax.ShapeDtypeStruct((1, BASIS), f32), jax.ShapeDtypeStruct((1, FIXES), f32)),
        in_specs=[pl.BlockSpec(memory_space=pltpu.HBM)] * 8 + [SMEM],
        out_specs=(VMEM, VMEM),
        scratch_shapes=[
            pltpu.VMEM((6, 1, FIXES), i32),
            pltpu.VMEM((16, LAYERS, 256), bf16),
            pltpu.VMEM((1, BASIS), f32),
            pltpu.VMEM((OWNERS, 1, 128), f32),
            pltpu.VMEM((OWNERS, 1, 128), f32),
            pltpu.VMEM((128, 128), f32),
            pltpu.VMEM((1024, 256), bf16),
            pltpu.VMEM((BASIS, served), bf16),
            pltpu.VMEM((BASIS, served), bf16),
            pltpu.VMEM((16, served), bf16),
            pltpu.VMEM((LAYERS, served), i32),
            pltpu.VMEM((2 * GROUP, ROWS, 128), f32),
            chunks, chunks, chunks,
            chunk,
            pltpu.VMEM((LEVELS, ROWS, 128), f32),
            chunk,
            pltpu.VMEM((2 * GROUP, ROWS, 128), f32),
            pltpu.VMEM((OWNERS, 6, 128), i32),
            pltpu.VMEM((OWNERS, 6, 128), i32),
            pltpu.VMEM((128, served), bf16),
            pltpu.VMEM((BASIS, FIXES), bf16),
            pltpu.VMEM((1, FIXES), f32),
            pltpu.VMEM((4, 128, BASIS + 128), f32),
            pltpu.VMEM((768, BASIS + 128), bf16),
            pltpu.SemaphoreType.DMA((8,)),
            one, one, one, one,
            one, group, one, one, deep, deep, group, group, one, one,
        ],
        compiler_params=pltpu.CompilerParams(collective_id=0, has_side_effects=True, vmem_limit_bytes=LIMIT),
    )(*lines, raster, beta, smooth)


def shards(owner, tile_local, anchor, frac_x, frac_y, label, raster, beta, smooth):
    lines = [array.reshape(1, FIXES) for array in (owner, tile_local, anchor, frac_x, frac_y, label)]
    beta_new, eta_new = step(lines, raster, beta.reshape(1, BASIS), smooth)
    return beta_new.reshape(BASIS), eta_new.reshape(FIXES)


def solution(mesh):
    fixes = P(("tile", "rep"))
    placed = (P(("tile", "rep"), None), fixes, fixes, fixes, fixes, fixes, P("tile", None, None), P(), P())
    return jax.shard_map(shards, mesh=mesh, in_specs=placed, out_specs=(P(), fixes), check_vma=False)
```

time: 111 us -> 96 us (0.86)
  Pallas kernels: 108 us -> 93.3 us
    pallas_call x2 -> x1, Pallas kernels: 108 us -> 93.3 us  [step(): pl.pallas_call(step_kernel, out_shape=(jax.ShapeDtypeStruct((1, BASIS), f...]
    unnamed x2 -> x6, local copies, waits for them, and re-layouts: 2.49 us -> 1.89 us
where the time goes in v3:
time: 96 us; the launch traced here: 95.8 us
  Pallas kernels  93.3 us (97%)
  local copies, waits for them, and re-layouts  1.89 us (2%)
    pallas_call x1, Pallas kernels, step(): pl.pallas_call(step_kernel, out_shape=(jax.ShapeDtypeStruct((1, BASIS), f...  93.3 us

profile of v3, /device:TPU:1, one launch (start us, length us, event | category | flops | bytes accessed | tf_op | source)
XLA Modules:
  0.0 95.8 jit_solution(6651891411806563582)
XLA Ops:
  0.6 93.3 %shard_map.104 = (f32[1,512]{1,0:T(1,128)}, f32[1,512]{1,0:T(1,128)}) custom-call(s32[1,512]{1,0:T(1,128)} %bitcast.9, s32[1,512]{1,0:T(1,128)} %bitcast.10, s32[1,512]{1,0:T(1,128)} %bitcast.11, s32[1,512]{1,0:T(1,128)} %bitcast.12, s32[1,512]{1,0:T(1,128)} %bitcast.13, s32[1,512]{1,0:T(1,128)} %bitcast.14, bf16[16,64,256]{2,1,0:T(8,128)(2,1)} %raster.1, ...), custom_call_target="tpu_custom_call" | custom-call | tf_op jit(solution)/shard_map/pallas_call | solution.py:495
  93.9 0.0 copy-start.1
  93.9 0.7 copy-done.1
  94.6 0.0 copy-start
  94.6 0.6 copy.13
  95.2 0.1 copy-done
  95.2 0.6 copy.14
Async XLA Ops:
  93.9 0.7 copy-start.1
  94.6 0.7 copy-start

commit v4 on v3

--- a/solution.py
+++ b/solution.py
@@ -20,6 +20,7 @@
 ROWS = 24
 GRAM_TILES = 160
 TARGET_ROW = GRAM_TILES % 3 * 8
+FIRST = 3
 REACH = 2.5
 STEPS = 13104.0
 MESH = pl.DeviceIdType.MESH
@@ -46,6 +47,12 @@
     mid = rest.astype(jnp.bfloat16)
     low = (rest - mid.astype(jnp.float32)).astype(jnp.bfloat16)
     return high, mid, low
+
+
+def add_tree(terms):
+    while len(terms) > 1:
+        terms = [terms[k] + terms[k + 1] if k + 1 < len(terms) else terms[k] for k in range(0, len(terms), 2)]
+    return terms[0]
 
 
 def stacked_thirds(x):
@@ -78,22 +85,22 @@
     return dot(named_b, spread, NT), slot
 
 
+def other_owners(tile):
+    x, z = lax.div(tile, DEEP), lax.rem(tile, DEEP)
+    reach = lambda step, size: min(step, size - step)
+    steps = [(dx, dz) for dx in range(4) for dz in range(DEEP) if dx or dz]
+    for dx, dz in sorted(steps, key=lambda step: -(reach(step[0], 4) + reach(step[1], DEEP))):
+        yield lax.rem(x + dx, 4) * DEEP + lax.rem(z + dz, DEEP)
+
+
 def greet_tile(barrier, tile, rep):
-    def greet(step, _):
-        pl.semaphore_signal(barrier, inc=1, device_id=(lax.rem(tile + step, OWNERS), rep), device_id_type=MESH)
-        return 0
-
-    lax.fori_loop(1, OWNERS, greet, 0)
-
-
-def send_all(tile, rep, out, came, send_sem, recv_sem):
-    def begin(step, _):
-        peer = lax.rem(tile + step, OWNERS)
+    for peer in other_owners(tile):
+        pl.semaphore_signal(barrier, inc=1, device_id=(peer, rep), device_id_type=MESH)
+
+
+def send_some(peers, tile, rep, out, came, send_sem, recv_sem):
+    for peer in peers:
         remote(out.at[peer], came.at[tile], send_sem, recv_sem, (peer, rep)).start()
-        return 0
-
-    lax.fori_loop(1, OWNERS, begin, 0)
-    came[tile] = out[tile]
 
 
 def all_messages(tile, rep, out, came, send_sem, recv_sem):
@@ -126,7 +133,7 @@
     return (bump * bump * bump).reshape(BASIS, values.shape[1]).astype(jnp.bfloat16)
 
 
-def form_terms(codes, beta, packed, coded, rows_out, turned, scaled, resid):
+def form_terms(codes, beta, packed, coded, rows_out, turned, scaled, resid, panel_done):
     beta_parts = stacked_thirds(beta[...])
 
     def block(at):
@@ -170,85 +177,96 @@
             for r in range(16):
                 packed[tile // 3, tile % 3 * 8:tile % 3 * 8 + 8, :] = panel[r * 8:r * 8 + 8, (j - i) * 128:(j - i + 1) * 128]
                 tile += 1
-
-
-def add_up(place, packed, mate_in, paired, group_in, mine, level_in, whole, result, sems, while_down, while_back):
+        panel_done(tile // 6 if i < 3 else GROUP)
+
+
+def add_up(place, packed, mate_in, paired, group_in, mine, level_in, whole, result, sems, while_down):
     s_mate, r_mate, s_group, r_group, s_level, r_level, s_wide, r_wide, s_last, r_last = sems
     me, core, pair, mate, chip, level = place
     peer = chip(lax.rem(me + 1, GROUP))
     most = pl.ds(0, GROUP - 1)
+    others = [lax.rem(pair + step, LEVELS) for step in (4, 3, 5, 2, 6, 1, 7)]
+    around = [lax.rem(me + step, GROUP) for step in range(1, GROUP)]
+    sent = [0]
 
     def to_mate(p):
-        return remote(packed.at[(1 - core) * GROUP + p], mate_in.at[p], s_mate, r_mate.at[p], mate)
+        return remote(packed.at[2 * p + 1 - core], mate_in.at[p], s_mate, r_mate.at[p], mate)
 
     def back_chip(p, slot):
-        return remote(whole, result.at[core * GROUP + slot], s_wide.at[p], r_wide.at[slot], chip(p))
-
-    def back_mate(p):
-        at = core * GROUP + p
-        return remote(result.at[at], result.at[at], s_last, r_last, mate)
-
-    def each(body, first=1, last=GROUP):
-        def step(k, _):
-            body(lax.rem(me + k, GROUP))
-            return 0
-
-        lax.fori_loop(first, last, step, 0)
-
-    each(lambda p: to_mate(p).start(), 1, GROUP + 1)
+        return remote(whole, result.at[2 * slot + core], s_wide, r_wide.at[slot], chip(p))
+
+    def back_mate(p, whose):
+        chunk = result.at[2 * p + whose]
+        return remote(chunk, chunk, s_last, r_last.at[p], mate)
+
+    def all_group():
+        return remote(paired.at[most], group_in.at[most], s_group, r_group, peer)
+
+    def send_ready(stop):
+        for p in range(sent[0], stop):
+            to_mate(p).start()
+        sent[0] = stop
 
     def pair_sum(p):
         to_mate(p).wait_recv()
-        paired[p] = packed[core * GROUP + p] + mate_in[p]
-
-    def pair_and_send(p):
-        pair_sum(p)
-        remote(paired.at[p], group_in.at[me], s_group, r_group, chip(p)).start()
-
-    each(pair_and_send)
-    pair_sum(me)
-    group_in[me] = paired[me]
-    while_down()
-    all_group = remote(paired.at[most], group_in.at[most], s_group, r_group, peer)
-    all_group.wait_recv()
-
-    def gather(k, total):
-        return total + (group_in[4 * k] + group_in[4 * k + 1]) + (group_in[4 * k + 2] + group_in[4 * k + 3])
-
-    mine[...] = lax.fori_loop(0, GROUP // 4, gather, jnp.zeros((ROWS, 128), jnp.float32))
-    others = [lax.rem(pair + step, LEVELS) for step in (4, 3, 5, 2, 6, 1, 7)]
-    for k in others:
-        remote(mine, level_in.at[pair], s_level.at[k], r_level.at[pair], level(k)).start()
-    level_in[pair] = mine[...]
-    for k in others:
-        remote(mine, level_in.at[k], s_level.at[k], r_level.at[k], level(k)).wait_recv()
-    total = level_in[0]
-    for k in range(1, LEVELS):
-        total = total + level_in[k]
-    whole[...] = total
-
-    each(lambda p: back_chip(p, me).start())
-    result[core * GROUP + me] = total
-    back_mate(me).start()
-    while_back()
+        paired[p] = packed[2 * p + core] + mate_in[p]
 
     def forward(p):
-        back_chip(p, p).wait_recv()
-        back_mate(p).start()
-
-    each(forward)
-    theirs = result.at[pl.ds((1 - core) * GROUP, GROUP)]
-    remote(theirs, theirs, s_last, r_last, mate).wait_recv()
+        @pl.when(p != me)
+        def _():
+            back_chip(p, p).wait_recv()
+            back_mate(p, core).start()
+
+    def down_and_first(first):
+        for p in around:
+            pair_sum(p)
+            remote(paired.at[p], group_in.at[me], s_group, r_group, chip(p)).start()
+        pair_sum(me)
+        group_in[me] = paired[me]
+        while_down()
+        all_group().wait_recv()
+        mine[...] = add_tree([group_in[p] for p in range(GROUP)])
+        for k in others:
+            remote(mine, level_in.at[pair], s_level.at[k], r_level.at[pair], level(k)).start()
+        level_in[pair] = mine[...]
+        for k in others:
+            remote(mine, level_in.at[k], s_level.at[k], r_level.at[k], level(k)).wait_recv()
+        total = add_tree([level_in[k] for k in range(LEVELS)])
+        whole[...] = total
+        result[2 * me + core] = total
+        for p in around:
+            back_chip(p, me).start()
+        back_mate(me, core).start()
+        for p in range(first):
+            forward(p)
+        for p in range(first):
+            back_mate(p, 1 - core).wait_recv()
+
+    def forward_rest(start, stop):
+        def one(p, _):
+            forward(p)
+            return 0
+
+        lax.fori_loop(start, stop, one, 0)
+
+    def wait_rest(start):
+        def one(p, _):
+            back_mate(p, 1 - core).wait_recv()
+            return 0
+
+        lax.fori_loop(start, GROUP, one, 0)
 
     def settle():
         remote(mate_in, mate_in, s_mate, s_mate, mate).wait_send()
-        all_group.wait_send()
+        all_group().wait_send()
         for k in others:
             remote(mine, level_in.at[k], s_level.at[k], r_level.at[k], level(k)).wait_send()
-        each(lambda p: back_chip(p, me).wait_send())
-        remote(theirs, theirs, s_last, r_last, mate).wait_send()
-
-    return settle
+        some = result.at[most]
+        remote(some, some, s_wide, s_wide, peer).wait_send()
+        half = result.at[pl.ds(0, GROUP)]
+        remote(half, half, s_last, s_last, mate).wait_send()
+
+    return send_ready, down_and_first, forward_rest, wait_rest, settle
 
 
 def pack_values(coded, out):
@@ -285,12 +303,6 @@
 def reciprocal(x):
     guess = pltpu.reciprocal(x, approx=True)
     return guess * (2.0 - x * guess)
-
-
-def add_tree(terms):
-    while len(terms) > 1:
-        terms = [terms[k] + terms[k + 1] if k + 1 < len(terms) else terms[k] for k in range(0, len(terms), 2)]
-    return terms[0]
 
 
 def six_left(x):
@@ -362,23 +374,27 @@
     return inner
 
 
-def solve_system(sums, smooth, beta_new, system, spread, late_chores):
+def solve_system(sums, smooth, beta_new, system, spread, first_chores, late_chores):
     count = 1.0 / (FIXES * 512.0)
     lane, row = iota((8, 128), 1), iota((8, 128), 0)
     inner = second_difference()
-    tile = 0
-    for i, j in BLOCKS:
+
+    def assemble(number):
+        i, j = BLOCKS[number]
         for r in range(16):
+            tile = 16 * number + r
             value = sums[tile // 3, tile % 3 * 8:tile % 3 * 8 + 8, :] * count
             if i == j:
                 value = value + jnp.where(lane // 8 == r, smooth[16 * i + r] * inner, 0.0)
                 value = value + jnp.where(lane == row + 8 * r, RIDGE, 0.0)
             system[i, r * 8:r * 8 + 8, j * 128:(j + 1) * 128] = value
-            tile += 1
-    for part in range(4):
-        line = sums[GRAM_TILES // 3, TARGET_ROW + part:TARGET_ROW + part + 1, :] * count
-        system[part, :, 512:640] = jnp.broadcast_to(line, (128, 128)).T
-
+
+    def assemble_right():
+        for part in range(4):
+            line = sums[GRAM_TILES // 3, TARGET_ROW + part:TARGET_ROW + part + 1, :] * count
+            system[part, :, 512:640] = jnp.broadcast_to(line, (128, 128)).T
+
+    assemble(0)
     def spread_of(k, inverse, start, stop):
         part = dot(inverse, six_right(system[k, :, start:stop]))
         system[k, :, start:stop] = part
@@ -387,7 +403,7 @@
     def eliminate(i, left, start, stop):
         system[i, :, start:stop] = system[i, :, start:stop] - dot(left, spread[:, start:stop])
 
-    pending = []
+    pending = first_chores + [functools.partial(assemble, number) for number in range(1, 10)] + [assemble_right]
     for k in range(4):
         diagonal = [system[k, r * 8:r * 8 + 8, k * 128:(k + 1) * 128] for r in range(16)]
         inverse = six_left(jnp.concatenate(invert(diagonal, pending), axis=0))
@@ -461,25 +477,38 @@
     pl.semaphore_wait(barrier, OWNERS - 1 + 24 + 1)
 
     codes_sent = (tile, rep, out_codes, came, send_codes, recv_codes)
-    send_all(*codes_sent)
+    came[tile] = out_codes[tile]
+    send_some(other_owners(tile), *codes_sent)
     all_messages(*codes_sent).wait_recv()
     arrived = jnp.concatenate([came[k] for k in range(OWNERS)], axis=0)
     codes[...] = jnp.concatenate([arrived, pltpu.roll(arrived, 128 - 12, 1)], axis=0).T
-    form_terms(codes, beta_in, packed, coded, rows, turned, scaled, resid)
-
     values_sent = (tile, rep, out_values, came_values, send_values, recv_values)
-    settle = add_up(
+    send_ready, down_and_first, forward_rest, wait_rest, settle = add_up(
         (me, core, pair, mate, chip, level), packed, mate_in, paired, group_in, mine, level_in, whole, result, sems,
-        lambda: pack_values(coded, out_values), lambda: send_all(*values_sent))
+        lambda: pack_values(coded, out_values))
+    form_terms(codes, beta_in, packed, coded, rows, turned, scaled, resid, send_ready)
+    down_and_first(FIRST)
 
     def place_rows(part):
         values = values_of_fixes(value_bytes, lines[0, :, part * 128:(part + 1) * 128], slot_row[:, part * 128:(part + 1) * 128])
         own_rows[:, part * 128:(part + 1) * 128] = expand(values)
 
-    chores = [settle, lambda: all_messages(*codes_sent).wait_send(), lambda: all_messages(*values_sent).wait_recv()]
+    peers = list(other_owners(tile))
+    half = (FIRST + GROUP) // 2
+    first_chores = [functools.partial(forward_rest, FIRST, half), functools.partial(forward_rest, half, GROUP)]
+    first_chores += [functools.partial(send_some, peers[k:k + 21], *values_sent) for k in range(0, OWNERS - 1, 21)]
+    first_chores += [functools.partial(wait_rest, FIRST)]
+
+    def settle_all():
+        settle()
+        all_messages(*codes_sent).wait_send()
+        came_values[tile] = out_values[tile]
+        all_messages(*values_sent).wait_recv()
+
+    chores = [settle_all]
     chores += [functools.partial(unpack_words, came_values, value_bytes, t) for t in range(3)]
     chores += [functools.partial(place_rows, part) for part in range(4)]
-    solve_system(result, smooth, beta_new, system, spread, chores)
+    solve_system(result, smooth, beta_new, system, spread, first_chores, chores)
     eta_new[...] = jnp.sum(dot(stacked_thirds(beta_new[...]), own_rows[...]), axis=0, keepdims=True)
     all_messages(*values_sent).wait_send()
 
@@ -524,7 +553,7 @@
             pltpu.VMEM((768, BASIS + 128), bf16),
             pltpu.SemaphoreType.DMA((8,)),
             one, one, one, one,
-            one, group, one, one, deep, deep, group, group, one, one,
+            one, group, one, one, deep, deep, one, group, one, group,
         ],
         compiler_params=pltpu.CompilerParams(collective_id=0, has_side_effects=True, vmem_limit_bytes=LIMIT),
     )(*lines, raster, beta, smooth)

time: 96 us -> 89.4 us (0.931)
  Pallas kernels: 93.3 us -> 86.6 us
    pallas_call x1, Pallas kernels: 93.3 us -> 86.6 us  [step(): pl.pallas_call(step_kernel, out_shape=(jax.ShapeDtypeStruct((1, BASIS), f...]
where the time goes in v4:
time: 89.4 us; the launch traced here: 89.1 us
  Pallas kernels  86.6 us (97%)
  local copies, waits for them, and re-layouts  1.89 us (2%)
    pallas_call x1, Pallas kernels, step(): pl.pallas_call(step_kernel, out_shape=(jax.ShapeDtypeStruct((1, BASIS), f...  86.6 us
    unnamed x6, local copies, waits for them, and re-layouts  1.89 us

profile of v4, /device:TPU:1, one launch (start us, length us, event | category | flops | bytes accessed | tf_op | source)
XLA Modules:
  0.0 89.1 jit_solution(7956727480737816042)
XLA Ops:
  0.6 86.6 %shard_map.104 = (f32[1,512]{1,0:T(1,128)}, f32[1,512]{1,0:T(1,128)}) custom-call(s32[1,512]{1,0:T(1,128)} %bitcast.9, s32[1,512]{1,0:T(1,128)} %bitcast.10, s32[1,512]{1,0:T(1,128)} %bitcast.11, s32[1,512]{1,0:T(1,128)} %bitcast.12, s32[1,512]{1,0:T(1,128)} %bitcast.13, s32[1,512]{1,0:T(1,128)} %bitcast.14, bf16[16,64,256]{2,1,0:T(8,128)(2,1)} %raster.1, ...), custom_call_target="tpu_custom_call" | custom-call | tf_op jit(solution)/shard_map/pallas_call | solution.py:524
  87.2 0.0 copy-start.1
  87.2 0.7 copy-done.1
  87.9 0.0 copy-start
  87.9 0.6 copy.13
  88.5 0.1 copy-done
  88.5 0.6 copy.14
Async XLA Ops:
  87.2 0.7 copy-start.1
  87.9 0.7 copy-start

commit v5 on v4

--- a/solution.py
+++ b/solution.py
@@ -20,6 +20,7 @@
 ROWS = 24
 GRAM_TILES = 160
 TARGET_ROW = GRAM_TILES % 3 * 8
+USED = 27
 FIRST = 3
 REACH = 2.5
 STEPS = 13104.0
@@ -152,7 +153,7 @@
             term = weight_y * along[r * 64:(r + 1) * 64]
             values = term if values is None else values + term
         values = values * (1.0 / 65536.0)
-        lanes = pl.ds(pl.multiple_of(at * 256, 256), 256)
+        lanes = pl.ds(at * 256, 256)
         coded[:, lanes] = jnp.floor(jnp.clip(values, -REACH, REACH) * STEPS + 0.5).astype(jnp.int32)
         rows = expand(values)
         rows_out[:, lanes] = rows
@@ -164,9 +165,10 @@
         scaled[:, lanes] = (jnp.sqrt(weight) * rows.astype(jnp.float32)).astype(jnp.bfloat16)
         resid[:, lanes] = stacked_thirds(weight * eta + (outcome - prob) * live)
 
-    pl.loop(0, 6)(block)
+    for at in range(6):
+        block(at)
     target = jnp.sum(dot(resid[...], rows_out[...], NT), axis=0, keepdims=True)
-    for spare in range(GRAM_TILES, 2 * GROUP * 3):
+    for spare in range(GRAM_TILES, 2 * USED * 3):
         packed[spare // 3, spare % 3 * 8:spare % 3 * 8 + 8, :] = jnp.zeros((8, 128), jnp.float32)
     for part in range(4):
         packed[GRAM_TILES // 3, TARGET_ROW + part:TARGET_ROW + part + 1, :] = target[:, part * 128:(part + 1) * 128]
@@ -203,7 +205,7 @@
         return remote(paired.at[most], group_in.at[most], s_group, r_group, peer)
 
     def send_ready(stop):
-        for p in range(sent[0], stop):
+        for p in range(sent[0], min(stop, USED)):
             to_mate(p).start()
         sent[0] = stop
 
@@ -217,26 +219,40 @@
             back_chip(p, p).wait_recv()
             back_mate(p, core).start()
 
+    def to_chip(p):
+        return remote(paired.at[p], group_in.at[me], s_group, r_group, chip(p))
+
     def down_and_first(first):
-        for p in around:
+        for step in range(1, USED):
+            p = lax.rem(me + step, USED)
             pair_sum(p)
-            remote(paired.at[p], group_in.at[me], s_group, r_group, chip(p)).start()
-        pair_sum(me)
-        group_in[me] = paired[me]
+            to_chip(p).start()
+        last = lax.rem(me, USED)
+        pair_sum(last)
+
+        @pl.when(me >= USED)
+        def _():
+            to_chip(last).start()
+
         while_down()
-        all_group().wait_recv()
-        mine[...] = add_tree([group_in[p] for p in range(GROUP)])
-        for k in others:
-            remote(mine, level_in.at[pair], s_level.at[k], r_level.at[pair], level(k)).start()
-        level_in[pair] = mine[...]
-        for k in others:
-            remote(mine, level_in.at[k], s_level.at[k], r_level.at[k], level(k)).wait_recv()
-        total = add_tree([level_in[k] for k in range(LEVELS)])
-        whole[...] = total
-        result[2 * me + core] = total
-        for p in around:
-            back_chip(p, me).start()
-        back_mate(me, core).start()
+
+        @pl.when(me < USED)
+        def _():
+            group_in[me] = paired[me]
+            all_group().wait_recv()
+            mine[...] = add_tree([group_in[p] for p in range(GROUP)])
+            for k in others:
+                remote(mine, level_in.at[pair], s_level.at[k], r_level.at[pair], level(k)).start()
+            level_in[pair] = mine[...]
+            for k in others:
+                remote(mine, level_in.at[k], s_level.at[k], r_level.at[k], level(k)).wait_recv()
+            total = add_tree([level_in[k] for k in range(LEVELS)])
+            whole[...] = total
+            result[2 * me + core] = total
+            for p in around:
+                back_chip(p, me).start()
+            back_mate(me, core).start()
+
         for p in range(first):
             forward(p)
         for p in range(first):
@@ -254,17 +270,26 @@
             back_mate(p, 1 - core).wait_recv()
             return 0
 
-        lax.fori_loop(start, GROUP, one, 0)
+        lax.fori_loop(start, USED, one, 0)
+
+    def sent_bytes(count, sem):
+        some = result.at[pl.ds(0, count)]
+        remote(some, some, sem, sem, peer).wait_send()
 
     def settle():
-        remote(mate_in, mate_in, s_mate, s_mate, mate).wait_send()
-        all_group().wait_send()
-        for k in others:
-            remote(mine, level_in.at[k], s_level.at[k], r_level.at[k], level(k)).wait_send()
-        some = result.at[most]
-        remote(some, some, s_wide, s_wide, peer).wait_send()
-        half = result.at[pl.ds(0, GROUP)]
-        remote(half, half, s_last, s_last, mate).wait_send()
+        sent_bytes(USED, s_mate)
+        sent_bytes(USED - 1, s_group)
+        sent_bytes(USED, s_last)
+
+        @pl.when(me >= USED)
+        def _():
+            sent_bytes(1, s_group)
+
+        @pl.when(me < USED)
+        def _():
+            for k in others:
+                remote(mine, level_in.at[k], s_level.at[k], r_level.at[k], level(k)).wait_send()
+            sent_bytes(GROUP - 1, s_wide)
 
     return send_ready, down_and_first, forward_rest, wait_rest, settle
 
@@ -346,16 +371,9 @@
             lead = sweep(lead)
             columns = columns[:m + 2] + later
         taken = [take(lead, m) for m in range(8)]
-        order = [(b + 1 + s) % 16 for s in range(15)]
-        far = order[8:]
-        left = jnp.concatenate([jnp.where(inside, tiles[i], 0.0) for i in far], axis=0)
-        blank = lambda n: [jnp.zeros((8 * n, 128), jnp.float32)] if n else []
-        change = dot(six_left(left), six_right(jnp.concatenate(blank(b) + [lead] + blank(15 - b), axis=0)))
-        for i in order[:8]:
+        for i in [(b + 1 + s) % 16 for s in range(15)]:
             terms = [column(tiles[i], 8 * b + m) * taken[m] for m in range(8)]
             tiles[i] = jnp.where(inside, 0.0, tiles[i]) - add_tree(terms)
-        for s, i in enumerate(far):
-            tiles[i] = jnp.where(inside, 0.0, tiles[i]) - change[8 * s:8 * s + 8, :]
         tiles[b] = lead
         for chore in chores[b * share:(b + 1) * share]:
             chore()
@@ -494,8 +512,8 @@
         own_rows[:, part * 128:(part + 1) * 128] = expand(values)
 
     peers = list(other_owners(tile))
-    half = (FIRST + GROUP) // 2
-    first_chores = [functools.partial(forward_rest, FIRST, half), functools.partial(forward_rest, half, GROUP)]
+    half = (FIRST + USED) // 2
+    first_chores = [functools.partial(forward_rest, FIRST, half), functools.partial(forward_rest, half, USED)]
     first_chores += [functools.partial(send_some, peers[k:k + 21], *values_sent) for k in range(0, OWNERS - 1, 21)]
     first_chores += [functools.partial(wait_rest, FIRST)]
 

time: 89.4 us -> 82 us (0.917)
  Pallas kernels: 86.6 us -> 79.2 us
    pallas_call x1, Pallas kernels: 86.6 us -> 79.2 us  [step(): pl.pallas_call(step_kernel, out_shape=(jax.ShapeDtypeStruct((1, BASIS), f...]
where the time goes in v5:
time: 82 us; the launch traced here: 81.8 us
  Pallas kernels  79.2 us (97%)
  local copies, waits for them, and re-layouts  1.89 us (2%)
    pallas_call x1, Pallas kernels, step(): pl.pallas_call(step_kernel, out_shape=(jax.ShapeDtypeStruct((1, BASIS), f...  79.2 us
    unnamed x6, local copies, waits for them, and re-layouts  1.89 us

profile of v5, /device:TPU:1, one launch (start us, length us, event | category | flops | bytes accessed | tf_op | source)
XLA Modules:
  0.0 81.8 jit_solution(13748435853547551609)
XLA Ops:
  0.6 79.2 %shard_map.104 = (f32[1,512]{1,0:T(1,128)}, f32[1,512]{1,0:T(1,128)}) custom-call(s32[1,512]{1,0:T(1,128)} %bitcast.9, s32[1,512]{1,0:T(1,128)} %bitcast.10, s32[1,512]{1,0:T(1,128)} %bitcast.11, s32[1,512]{1,0:T(1,128)} %bitcast.12, s32[1,512]{1,0:T(1,128)} %bitcast.13, s32[1,512]{1,0:T(1,128)} %bitcast.14, bf16[16,64,256]{2,1,0:T(8,128)(2,1)} %raster.1, ...), custom_call_target="tpu_custom_call" | custom-call | tf_op jit(solution)/shard_map/pallas_call | solution.py:542
  79.9 0.0 copy-start.1
  79.9 0.7 copy-done.1
  80.5 0.0 copy-start
  80.5 0.6 copy.13
  81.1 0.1 copy-done
  81.2 0.6 copy.14
Async XLA Ops:
  79.9 0.7 copy-start.1
  80.5 0.7 copy-start

commit v6 on v5

--- a/solution.py
+++ b/solution.py
@@ -448,7 +448,7 @@
 
 
 def step_kernel(owner, local, anchor, frac_x, frac_y, label, raster, beta, smooth, beta_new, eta_new,
-                lines, raster_in, beta_in, out_codes, came, codes, turned, rows, scaled, resid, coded,
+                lines, raster_in, beta_in, smooth_in, out_codes, came, codes, turned, rows, scaled, resid, coded,
                 packed, mate_in, paired, group_in, mine, level_in, whole, result,
                 out_values, came_values, value_bytes, own_rows, slot_row, system, spread,
                 loads, send_codes, recv_codes, send_values, recv_values, *sems):
@@ -479,7 +479,7 @@
     lax.fori_loop(0, 24, greet, 0)
 
     arguments = [(source, lines.at[k]) for k, source in enumerate((owner, local, anchor, frac_x, frac_y, label))]
-    arguments += [(raster, raster_in), (beta, beta_in)]
+    arguments += [(raster, raster_in), (beta, beta_in), (smooth, smooth_in)]
     copies = [pltpu.make_async_copy(source, target, loads.at[k]) for k, (source, target) in enumerate(arguments)]
     for copy in copies:
         copy.start()
@@ -491,6 +491,7 @@
         out_codes[k] = message[k:k + 1, :]
     copies[6].wait()
     copies[7].wait()
+    copies[8].wait()
     swap_rows_and_tiles(raster_in, turned)
     pl.semaphore_wait(barrier, OWNERS - 1 + 24 + 1)
 
@@ -526,7 +527,7 @@
     chores = [settle_all]
     chores += [functools.partial(unpack_words, came_values, value_bytes, t) for t in range(3)]
     chores += [functools.partial(place_rows, part) for part in range(4)]
-    solve_system(result, smooth, beta_new, system, spread, first_chores, chores)
+    solve_system(result, smooth_in, beta_new, system, spread, first_chores, chores)
     eta_new[...] = jnp.sum(dot(stacked_thirds(beta_new[...]), own_rows[...]), axis=0, keepdims=True)
     all_messages(*values_sent).wait_send()
 
@@ -542,12 +543,13 @@
     return pl.pallas_call(
         step_kernel,
         out_shape=(jax.ShapeDtypeStruct((1, BASIS), f32), jax.ShapeDtypeStruct((1, FIXES), f32)),
-        in_specs=[pl.BlockSpec(memory_space=pltpu.HBM)] * 8 + [SMEM],
+        in_specs=[pl.BlockSpec(memory_space=pltpu.HBM)] * 9,
         out_specs=(VMEM, VMEM),
         scratch_shapes=[
             pltpu.VMEM((6, 1, FIXES), i32),
             pltpu.VMEM((16, LAYERS, 256), bf16),
             pltpu.VMEM((1, BASIS), f32),
+            pltpu.SMEM((LAYERS,), f32),
             pltpu.VMEM((OWNERS, 1, 128), f32),
             pltpu.VMEM((OWNERS, 1, 128), f32),
             pltpu.VMEM((128, 128), f32),
@@ -569,7 +571,7 @@
             pltpu.VMEM((1, FIXES), f32),
             pltpu.VMEM((4, 128, BASIS + 128), f32),
             pltpu.VMEM((768, BASIS + 128), bf16),
-            pltpu.SemaphoreType.DMA((8,)),
+            pltpu.SemaphoreType.DMA((9,)),
             one, one, one, one,
             one, group, one, one, deep, deep, one, group, one, group,
         ],

time: 82 us -> 81.4 us (level)
  no operation moved by 1% of the time
where the time goes in v6:
time: 81.4 us; the launch traced here: 81.2 us
  Pallas kernels  78.7 us (97%)
  local copies, waits for them, and re-layouts  1.89 us (2%)
    pallas_call x1, Pallas kernels, step(): pl.pallas_call(step_kernel, out_shape=(jax.ShapeDtypeStruct((1, BASIS), f...  78.7 us
    unnamed x6, local copies, waits for them, and re-layouts  1.89 us

profile of v6, /device:TPU:1, one launch (start us, length us, event | category | flops | bytes accessed | tf_op | source)
XLA Modules:
  0.0 81.2 jit_solution(34177914553445118)
XLA Ops:
  0.6 78.7 %shard_map.104 = (f32[1,512]{1,0:T(1,128)}, f32[1,512]{1,0:T(1,128)}) custom-call(s32[1,512]{1,0:T(1,128)} %bitcast.9, s32[1,512]{1,0:T(1,128)} %bitcast.10, s32[1,512]{1,0:T(1,128)} %bitcast.11, s32[1,512]{1,0:T(1,128)} %bitcast.12, s32[1,512]{1,0:T(1,128)} %bitcast.13, s32[1,512]{1,0:T(1,128)} %bitcast.14, bf16[16,64,256]{2,1,0:T(8,128)(2,1)} %raster.1, ...), custom_call_target="tpu_custom_call" | custom-call | tf_op jit(solution)/shard_map/pallas_call | solution.py:543
  79.3 0.0 copy-start.1
  79.3 0.7 copy-done.1
  80.0 0.0 copy-start
  80.0 0.6 copy.13
  80.6 0.1 copy-done
  80.7 0.6 copy.14
Async XLA Ops:
  79.3 0.7 copy-start.1
  80.0 0.7 copy-start
